TPU v7x, 32 devices: a whole 2x2x4 slice. The times are simulated.
32 devices in a mesh: col: 8 (over z, x), row: 4 (over y, core).
Axes of the slice: x: 2, y: 2, z: 4, core: 2. Of those that a mesh axis runs over, the one named last changes fastest.
Arguments:
- returns: bfloat16 [4096, 2048], P(('row', 'col')), may hold values from -6 to 6
- counts: int32 [4096], P(('row', 'col')), may hold values from 0 to 4
- partner_shift: int32 [3], replicated, may hold values from 1 to 7
Outputs:
- blocks_out: float32 [4096, 2048], P('row', 'col')
- bounds: float32 [3], replicated
All inputs are finite; a program needn't handle non-finite values.
Results may differ from a plain program's by a relative error of at most 0.0003.
Values sent between devices are 32-bit elements; how exact they have to be, the bound alone decides.
No kernel may reach another device: no remote copies, remote signals or barrier semaphores. Data moves between devices by JAX's collectives and lax.ppermute only.
A program may use at most 128 MiB of HBM per device.

v0:
```python
import functools

import jax
import jax.numpy as jnp
from jax import lax
from jax.experimental import pallas as pl
from jax.experimental.pallas import tpu as pltpu
from jax.sharding import PartitionSpec as P

BW = 128
ROUNDS = 3
RADIX = 8
TILE = 8
LONG = 3 << 30
STEP = 256
F32 = jnp.float32


def split(x):
    high = x.astype(jnp.bfloat16)
    return high, (x - high.astype(F32)).astype(jnp.bfloat16)


def dot(a, b, dims=((1,), (0,))):
    one = functools.partial(
        lax.dot_general, dimension_numbers=(dims, ((), ())), preferred_element_type=F32
    )
    return one(a[0], b[0]) + (one(a[0], b[1]) + one(a[1], b[0]))


def dots(a, b, dims=((1,), (0,))):
    return dot(split(a), split(b), dims)


def unit():
    rows = lax.broadcasted_iota(jnp.int32, (BW, BW), 0)
    return (rows == lax.broadcasted_iota(jnp.int32, (BW, BW), 1)).astype(F32)


def polar(m, top):
    eye = unit()
    square = 1.0 / (1.0 + top)
    gram, product = square * (eye + m), None
    for turn in range(3):
        factor = 1.5 * eye - 0.5 * gram
        cut = split(factor)
        product = factor if product is None else dot(split(product), cut)
        if turn < 2:
            gram = dot(split(gram), split(dot(cut, cut)))
    return jnp.sqrt(square) * product


def steps(size, body):
    @pl.loop(0, size // STEP)
    def _(i):
        body(i * STEP, pl.ds(pl.multiple_of(i * STEP, STEP), STEP))


def gram_into(first, second, gram_ref):
    gram_ref[:BW] += dots(first, second, ((0,), (0,)))
    gram_ref[BW:BW + 1] += jnp.sum(first * first, 0, keepdims=True)
    gram_ref[BW + 1:BW + 2] += jnp.sum(second * second, 0, keepdims=True)


def gather_kernel(at_ref, *refs):
    blocks, (first_ref, second_ref, gram_ref) = refs[:-3], refs[-3:]
    days = blocks[0].shape[0]
    for i, block in enumerate(blocks):
        place = pl.ds(pl.multiple_of(at_ref[i] * days, TILE), days)
        first_ref[place] = block[:, :BW]
        second_ref[place] = block[:, BW:]
    gram_ref[...] = jnp.zeros_like(gram_ref)
    gram_into(first_ref[...], second_ref[...], gram_ref)


def couple_kernel(total_days, g0, g1, first, second, coupling_ref, measure_ref, early_ref):
    summed = g0[...] + g1[...]
    norms = jnp.sqrt(summed[BW:BW + 2] / total_days + 1e-06)
    across = jnp.broadcast_to(norms[1:2], (BW, BW))
    down = jnp.broadcast_to(norms[0:1], (BW, BW)).T
    coupling = summed[:BW] / (total_days * down * across)
    measure_ref[...] = jnp.full((TILE, BW), jnp.sum(coupling * coupling), F32)
    coupling_ref[...] = coupling
    lead = early_ref.shape[0] - BW
    early_ref[:BW] = coupling
    early_ref[BW:] = dots(first[:lead], coupling) + second[:lead]


def late_mix_kernel(coupling, first, second, late_ref):
    lead = first.shape[0] - late_ref.shape[0]
    cut = split(coupling[...])

    def body(at, here):
        there = pl.ds(pl.multiple_of(lead + at, STEP), STEP)
        late_ref[here] = dot(split(first[there]), cut) + second[there]

    steps(late_ref.shape[0], body)


def keep_kernel(m0, m1, m2, m3, coupling, first, second, tops, first_ref, tops_ref):
    top = jnp.maximum(jnp.maximum(m0[...], m1[...]), jnp.maximum(m2[...], m3[...]))[:1]
    tops_ref[:1] = top
    tops_ref[1:] = tops[:TILE - 1]
    cut = split(coupling[...])
    factor = polar(dot(cut, cut, ((1,), (1,))), top)
    weight = split(factor)
    other = split(dot(cut, weight, ((0,), (0,))))

    def body(_, here):
        first_ref[here] = dot(split(first[here]), weight) - dot(split(second[here]), other)

    steps(first.shape[0], body)


def early_kernel(early, first, tops, factor_ref, second_ref, gram_ref):
    cut = split(early[:BW])
    factor = polar(dot(cut, cut, ((0,), (0,))), tops[:1])
    factor_ref[...] = factor
    weight = split(factor)
    gram_ref[...] = jnp.zeros_like(gram_ref)

    def body(at, here):
        there = pl.ds(pl.multiple_of(BW + at, BW), STEP)
        second_ref[here] = dot(split(early[there]), weight)
        gram_into(first[here], second_ref[here], gram_ref)

    steps(second_ref.shape[0], body)


def late_kernel(late, factor, first, lead, tops, first_ref, second_ref, gram_ref, tops_ref):
    second = dots(late[...], factor[...])
    size = lead.shape[0]
    first_ref[...] = first[...]
    tops_ref[...] = tops[...]
    second_ref[:size] = lead[...]
    second_ref[size:] = second
    gram_ref[...] = jnp.zeros_like(gram_ref)
    gram_into(first[size:], second, gram_ref)


def last_kernel(first, second, tops, out_ref, bounds_ref):
    out_ref[:, :BW] = first[...]
    out_ref[:, BW:] = second[...]
    for i in range(ROUNDS):
        bounds_ref[i] = tops[ROUNDS - 1 - i, 0]


def call(kernel, outs, *args, smem_in=0, smem_out=0, flops=0):
    vmem, smem = pl.BlockSpec(memory_space=pltpu.VMEM), pl.BlockSpec(memory_space=pltpu.SMEM)
    shapes = [jax.ShapeDtypeStruct(s, F32) for s in outs]
    return pl.pallas_call(
        kernel,
        out_shape=shapes,
        in_specs=[smem] * smem_in + [vmem] * (len(args) - smem_in),
        out_specs=[vmem] * (len(outs) - smem_out) + [smem] * smem_out,
        compiler_params=pltpu.CompilerParams(vmem_limit_bytes=24 << 20),
        cost_estimate=pl.CostEstimate(flops=flops, bytes_accessed=0, transcendentals=0) if flops else None,
    )(*args)


def forward(x, hop):
    n = lax.axis_size("col")
    return lax.ppermute(x, "col", [(i, (i + hop) % n) for i in range(n)])


def swapped(x, axis, mask):
    return lax.ppermute(x, axis, [(i, i ^ mask) for i in range(lax.axis_size(axis))])


def row_parts(x):
    return [x] + [swapped(x, "row", m) for m in range(1, lax.axis_size("row"))]


def halves(x):
    mask = 1
    while 2 * mask < lax.axis_size("row"):
        x = x + swapped(x, "row", mask)
        mask *= 2
    return x, swapped(x, "row", mask)


def most_of_col(x):
    n, rows = lax.axis_size("col"), lax.axis_size("row")
    mask = RADIX
    while mask < n:
        x = jnp.maximum(x, swapped(x, "col", mask))
        mask *= 2
    near = min(n, RADIX) - 1
    each = -(-near // rows)
    seen = []
    for j in range(each):
        route = [
            (c * rows + r, (c ^ min(1 + r * each + j, near)) * rows + r)
            for r in range(rows) for c in range(n)
        ]
        seen.append(lax.ppermute(x, ("col", "row"), route))
    return functools.reduce(jnp.maximum, seen, x)


def to_pairs(weighted):
    n = lax.axis_size("col")
    if n > RADIX:
        whole = lax.all_to_all(weighted, "col", split_axis=1, concat_axis=0, tiled=True)
        return [whole], jnp.zeros((1,), jnp.int32)
    me = lax.axis_index("col")
    days, width = weighted.shape[0], weighted.shape[1] // n
    blocks = []
    for mask in range(n):
        block = lax.dynamic_slice(weighted, (0, (me ^ mask) * width), (days, width))
        blocks.append(swapped(block, "col", mask) if mask else block)
    return blocks, me ^ jnp.arange(n, dtype=jnp.int32)


def on_device(returns, counts, partner_shift):
    n, rows = lax.axis_size("col"), lax.axis_size("row")
    total_days = returns.shape[0] * n * rows
    mine = total_days // rows
    weighted = returns.astype(F32) * jnp.sqrt(counts.astype(F32))[:, None]
    blocks, at = to_pairs(weighted)
    block, gram_shape, tile = (mine, BW), (BW + TILE, BW), (TILE, BW)
    lead = mine // 2
    first, second, gram = call(
        gather_kernel, [block, block, gram_shape], at, *blocks, smem_in=1
    )
    strides = [1]
    while strides[-1] * RADIX < n:
        strides.append(strides[-1] * RADIX)
    lowest = 1 if len(strides) == 1 else 0

    def settle(early, late, first, tops):
        factor, start, gram = call(
            early_kernel, [(BW, BW), (lead, BW), gram_shape], early, first, tops
        )
        first, second, rest, tops = call(
            late_kernel, [block, block, gram_shape, tile], late, factor, first, start, tops
        )
        return first, second, gram, rest, tops

    def move(hop, first, second, coupling, measure, early, tops):
        early = forward(early, hop) if hop else early
        late, = call(late_mix_kernel, [(mine - lead, BW)], coupling, first, second)
        late = forward(late, hop) if hop else late
        part = most_of_col(measure)
        kept, tops = call(
            keep_kernel, [block, tile], *row_parts(part), coupling, first, second, tops, flops=LONG
        )
        if len(strides) == 1:
            return settle(early, late, kept, tops)
        return kept, early, late, tops

    def joined(first, second, gram, rest, tops):
        return first, second, gram + rest, tops

    def one_round(carry, amount):
        first, second, gram, tops = carry
        coupling, measure, early = call(
            functools.partial(couple_kernel, float(total_days)), [(BW, BW), tile, (BW + lead, BW)],
            *halves(gram), first, second,
        )
        branches = [functools.partial(move, hop) for hop in range(lowest, min(n, RADIX))]
        moved = lax.switch(
            amount % RADIX - lowest, branches, first, second, coupling, measure, early, tops
        )
        if len(strides) == 1:
            return joined(*moved), None
        first, early, late, tops = moved
        for stride in strides[1:]:
            routes = [lambda *xs: xs] + [
                lambda *xs, hop=hop: tuple(forward(x, hop * stride) for x in xs)
                for hop in range(1, min(RADIX, n // stride))
            ]
            early, late = lax.switch(amount // stride % RADIX, routes, early, late)
        return joined(*settle(early, late, first, tops)), None

    tops = jnp.zeros(tile, F32)
    (first, second, _, tops), _ = lax.scan(one_round, (first, second, gram, tops), partner_shift)
    return tuple(
        call(last_kernel, [(mine, 2 * BW), (ROUNDS,)], first, second, tops, smem_out=1)
    )


def solution(mesh):
    placed = (P(("row", "col"), None), P(("row", "col")), P())
    return jax.shard_map(
        on_device, mesh=mesh, in_specs=placed, out_specs=(P("row", "col"), P()), check_vma=False
    )
```

profile of v0, /device:TPU:0, one launch (start us, length us, event | category | flops | bytes accessed | tf_op | source)
XLA Modules:
  0.0 124.8 jit_solution(165311972407506611)
XLA Ops:
  0.7 0.6 copy-done
  1.3 1.2 convert_multiply_fusion
  2.6 6.0 %collective-permute-start.57 = (f32[128,256]{1,0:T(8,128)S(1)}, f32[128,256]{1,0:T(8,128)S(1)}, u32[]{:S(2)}, u32[]{:S(2)}) collective-permute-start(f32[128,256]{1,0:T(8,128)S(1)} %get-tuple-element.303), channel_id=1, source_target_pairs={{0,28},{4,24},{8,20},{12,16},{16,12},{20,8},{24,4},{28,0},{1,29},{... | collective-permute-start | bytes 393224 | tf_op jit(solution)/shard_map/ppermute | solution.py:167
  8.9 0.8 collective-permute-start.55
  9.7 2.0 %collective-permute-start.54 = (f32[128,256]{1,0:T(8,128)S(1)}, f32[128,256]{1,0:T(8,128)S(1)}, u32[]{:S(2)}, u32[]{:S(2)}) collective-permute-start(f32[128,256]{1,0:T(8,128)S(1)} %get-tuple-element.306), channel_id=1, source_target_pairs={{0,16},{4,20},{8,24},{12,28},{16,0},{20,4},{24,8},{28,12},{1,17},{... | collective-permute-start | bytes 393224 | tf_op jit(solution)/shard_map/ppermute | solution.py:167
  11.7 2.3 %collective-permute-start.53 = (f32[128,256]{1,0:T(8,128)S(1)}, f32[128,256]{1,0:T(8,128)S(1)}, u32[]{:S(2)}, u32[]{:S(2)}) collective-permute-start(f32[128,256]{1,0:T(8,128)S(1)} %get-tuple-element.307), channel_id=1, source_target_pairs={{0,12},{4,8},{8,4},{12,0},{16,28},{20,24},{24,20},{28,16},{1,13},{... | collective-permute-start | bytes 393224 | tf_op jit(solution)/shard_map/ppermute | solution.py:167
  14.0 10.4 %collective-permute-start.52 = (f32[128,256]{1,0:T(8,128)S(1)}, f32[128,256]{1,0:T(8,128)S(1)}, u32[]{:S(2)}, u32[]{:S(2)}) collective-permute-start(f32[128,256]{1,0:T(8,128)S(1)} %get-tuple-element.308), channel_id=1, source_target_pairs={{0,8},{4,12},{8,0},{12,4},{16,24},{20,28},{24,16},{28,20},{1,9},{5... | collective-permute-start | bytes 393224 | tf_op jit(solution)/shard_map/ppermute | solution.py:167
  24.4 1.4 %collective-permute-start.51 = (f32[128,256]{1,0:T(8,128)S(1)}, f32[128,256]{1,0:T(8,128)S(1)}, u32[]{:S(2)}, u32[]{:S(2)}) collective-permute-start(f32[128,256]{1,0:T(8,128)S(1)} %get-tuple-element.309), channel_id=1, source_target_pairs={{0,4},{4,0},{8,12},{12,8},{16,20},{20,16},{24,28},{28,24},{1,5},{5... | collective-permute-start | bytes 393224 | tf_op jit(solution)/shard_map/ppermute | solution.py:167
  25.8 3.5 %collective-permute-done.55.refs_5_ = f32[128,256]{1,0:T(8,128)S(1)} collective-permute-done((f32[128,256]{1,0:T(8,128)S(1)}, f32[128,256]{1,0:T(8,128)S(1)}, u32[]{:S(2)}, u32[]{:S(2)}) %collective-permute-start.55) | collective-permute-done | bytes 131104 | tf_op jit(solution)/shard_map/ppermute | solution.py:167
  29.2 1.9 %collective-permute-done.54.refs_4_ = f32[128,256]{1,0:T(8,128)S(1)} collective-permute-done((f32[128,256]{1,0:T(8,128)S(1)}, f32[128,256]{1,0:T(8,128)S(1)}, u32[]{:S(2)}, u32[]{:S(2)}) %collective-permute-start.54) | collective-permute-done | bytes 131104 | tf_op jit(solution)/shard_map/ppermute | solution.py:167
  31.1 1.1 collective-permute-done.52.refs_2_
  32.2 1.0 shard_map.50
  33.9 89.8 %while.18 = (s32[]{:T(128)}, f32[1024,128]{1,0:T(8,128)S(1)}, f32[1024,128]{1,0:T(8,128)S(1)}, f32[136,128]{1,0:T(8,128)S(1)}, f32[8,128]{1,0:T(8,128)S(1)}, /*i...) while((s32[]{:T(128)}, f32[1024,128]{1,0:T(8,128)S(1)}, ...), condition=%wide.region_8.9_spmd, body=%wide.region_0.8_spmd.sunk | while | flops 3221262336 | bytes 3433162 | solution.py:276
  33.9 1.3 %collective-permute-done.49 = f32[136,128]{1,0:T(8,128)S(1)} collective-permute-done((f32[136,128]{1,0:T(8,128)S(1)}, f32[136,128]{1,0:T(8,128)S(1)}, u32[]{:S(2)}, u32[]{:S(2)}) %collective-permute-start.49) | collective-permute-done | bytes 69664 | tf_op jit(solution)/shard_map/while/body/eval_jaxpr/ppermute | solution.py:167
  35.2 1.6 %collective-permute-start.50 = (f32[136,128]{1,0:T(8,128)S(1)}, f32[136,128]{1,0:T(8,128)S(1)}, u32[]{:S(2)}, u32[]{:S(2)}) collective-permute-start(f32[136,128]{1,0:T(8,128)S(1)} %add.64.g0), channel_id=1, source_target_pairs={{0,2},{1,3},{2,0},{3,1},{4,6},{5,7},{6,4},{7,5},{8,10},{9,11},{10,... | collective-permute-start | bytes 208904 | tf_op jit(solution)/shard_map/while/body/eval_jaxpr/ppermute | solution.py:167
  39.9 20.2 %conditional.2 = (f32[1024,128]{1,0:T(8,128)S(1)}, f32[1024,128]{1,0:T(8,128)S(1)}, f32[136,128]{1,0:T(8,128)S(1)}, f32[136,128]{1,0:T(8,128)S(1)}, f32[8,128]{1,0:T(8,128)S(1)}) conditional(s32[]{:T(128)} %clamp.7, (f32[128,128]{1,0:T(8,128)S(1)}, f32[1024,128]{1,0:T(8,128)S(1)}, f32[1024,128]{1,0:T(8,128)S(1)}, ...), branch_computations={%region_1.1_spmd, %region_2.2_spmd, %region_3.3_spmd, %region_4.4_... | conditional | flops 3221227520 | bytes 2457920 | solution.py:261
  40.1 0.8 collective-permute-start.30
  40.8 3.5 %collective-permute-start.29 = (f32[640,128]{1,0:T(8,128)S(1)}, f32[640,128]{1,0:T(8,128)S(1)}, u32[]{:S(2)}, u32[]{:S(2)}) collective-permute-start(f32[640,128]{1,0:T(8,128)S(1)} %get-tuple-element.220), channel_id=1, source_target_pairs={{0,20},{4,24},{8,28},{12,0},{16,4},{20,8},{24,12},{28,16},{1,21},{... | collective-permute-start | bytes 983048 | tf_op jit(solution)/shard_map/while/body/eval_jaxpr/cond/branch_4_fun/ppermute | solution.py:163
  44.4 3.3 %collective-permute-start.34 = (f32[8,128]{1,0:T(8,128)S(1)}, f32[8,128]{1,0:T(8,128)S(1)}, u32[]{:S(2)}, u32[]{:S(2)}) collective-permute-start(f32[8,128]{1,0:T(8,128)S(1)} %maximum_maximum_fusion.4.m0), channel_id=1, source_target_pairs={{0,3},{1,2},{2,1},{3,0},{4,7},{5,6},{6,5},{7,4},{8,11},{9,10},{10,... | collective-permute-start | bytes 12296 | tf_op jit(solution)/shard_map/while/body/eval_jaxpr/cond/branch_4_fun/ppermute | solution.py:167
  47.7 1.7 %collective-permute-start.33 = (f32[8,128]{1,0:T(8,128)S(1)}, f32[8,128]{1,0:T(8,128)S(1)}, u32[]{:S(2)}, u32[]{:S(2)}) collective-permute-start(f32[8,128]{1,0:T(8,128)S(1)} %maximum_maximum_fusion.4.m0), channel_id=1, source_target_pairs={{0,2},{1,3},{2,0},{3,1},{4,6},{5,7},{6,4},{7,5},{8,10},{9,11},{10,... | collective-permute-start | bytes 12296 | tf_op jit(solution)/shard_map/while/body/eval_jaxpr/cond/branch_4_fun/ppermute | solution.py:167
  50.0 1.3 %collective-permute-done.33.m2 = f32[8,128]{1,0:T(8,128)S(1)} collective-permute-done((f32[8,128]{1,0:T(8,128)S(1)}, f32[8,128]{1,0:T(8,128)S(1)}, u32[]{:S(2)}, u32[]{:S(2)}) %collective-permute-start.33) | collective-permute-done | bytes 4128 | tf_op jit(solution)/shard_map/while/body/eval_jaxpr/cond/branch_4_fun/ppermute | solution.py:167
  51.3 2.3 %branch_4_fun.5 = (f32[1024,128]{1,0:T(8,128)S(1)}, f32[8,128]{1,0:T(8,128)S(1)}) custom-call(f32[8,128]{1,0:T(8,128)S(1)} %maximum_maximum_fusion.4.m0, f32[8,128]{1,0:T(8,128)S(1)} %collective-permute-done.32.m1, f32[8,128]{1,0:T(8,128)S(1)} %collective-permute-done.33.m2, f32[8,128]{1,0:T(8,128)S(1)} %collective-permute-done.34.m3, ...), custom_call_target="tpu_custom_call" | custom-call | flops 3221225472 | tf_op jit(solution)/shard_map/while/body/eval_jaxpr/cond/branch_4_fun/pallas_call | solution.py:151
  53.6 2.0 %branch_4_fun.6 = (f32[128,128]{1,0:T(8,128)S(1)}, f32[512,128]{1,0:T(8,128)S(1)}, f32[136,128]{1,0:T(8,128)S(1)}) custom-call(f32[640,128]{1,0:T(8,128)S(1)} %collective-permute-done.29.early, f32[1024,128]{1,0:T(8,128)S(1)} %get-tuple-element.223.first, f32[8,128]{1,0:T(8,128)S(1)} %get-tuple-element.224.tops), custom_call_target="tpu_custom_call" | custom-call | tf_op jit(solution)/shard_map/while/body/eval_jaxpr/cond/branch_4_fun/pallas_call | solution.py:151
  55.6 3.9 %collective-permute-done.28.late = f32[512,128]{1,0:T(8,128)S(1)} collective-permute-done((f32[512,128]{1,0:T(8,128)S(1)}, f32[512,128]{1,0:T(8,128)S(1)}, u32[]{:S(2)}, u32[]{:S(2)}) %collective-permute-start.28) | collective-permute-done | bytes 262176 | tf_op jit(solution)/shard_map/while/body/eval_jaxpr/cond/branch_4_fun/ppermute | solution.py:163
  60.2 1.2 collective-permute-done.49
  61.5 1.5 %collective-permute-start.50 = (f32[136,128]{1,0:T(8,128)S(1)}, f32[136,128]{1,0:T(8,128)S(1)}, u32[]{:S(2)}, u32[]{:S(2)}) collective-permute-start(f32[136,128]{1,0:T(8,128)S(1)} %add.64.g0), channel_id=1, source_target_pairs={{0,2},{1,3},{2,0},{3,1},{4,6},{5,7},{6,4},{7,5},{8,10},{9,11},{10,... | collective-permute-start | bytes 208904 | tf_op jit(solution)/shard_map/while/body/eval_jaxpr/ppermute | solution.py:167
  66.2 32.1 %conditional.2 = (f32[1024,128]{1,0:T(8,128)S(1)}, f32[1024,128]{1,0:T(8,128)S(1)}, f32[136,128]{1,0:T(8,128)S(1)}, f32[136,128]{1,0:T(8,128)S(1)}, f32[8,128]{1,0:T(8,128)S(1)}) conditional(s32[]{:T(128)} %clamp.7, (f32[128,128]{1,0:T(8,128)S(1)}, f32[1024,128]{1,0:T(8,128)S(1)}, f32[1024,128]{1,0:T(8,128)S(1)}, ...), branch_computations={%region_1.1_spmd, %region_2.2_spmd, %region_3.3_spmd, %region_4.4_... | conditional | flops 3221227520 | bytes 2457920 | solution.py:261
  66.3 10.8 %collective-permute-start.10 = (f32[8,128]{1,0:T(8,128)S(1)}, f32[8,128]{1,0:T(8,128)S(1)}, u32[]{:S(2)}, u32[]{:S(2)}) collective-permute-start(f32[8,128]{1,0:T(8,128)S(1)} %get-tuple-element.176), channel_id=1, source_target_pairs={{0,8},{4,12},{8,0},{12,4},{16,24},{20,28},{24,16},{28,20},{1,17},{... | collective-permute-start | bytes 12296 | tf_op jit(solution)/shard_map/while/body/eval_jaxpr/cond/branch_1_fun/ppermute | solution.py:196
  77.0 3.0 %collective-permute-start.9 = (f32[8,128]{1,0:T(8,128)S(1)}, f32[8,128]{1,0:T(8,128)S(1)}, u32[]{:S(2)}, u32[]{:S(2)}) collective-permute-start(f32[8,128]{1,0:T(8,128)S(1)} %get-tuple-element.176), channel_id=1, source_target_pairs={{0,4},{4,0},{8,12},{12,8},{16,20},{20,16},{24,28},{28,24},{1,13},{... | collective-permute-start | bytes 12296 | tf_op jit(solution)/shard_map/while/body/eval_jaxpr/cond/branch_1_fun/ppermute | solution.py:196
  80.1 1.9 %collective-permute-start.8 = (f32[640,128]{1,0:T(8,128)S(1)}, f32[640,128]{1,0:T(8,128)S(1)}, u32[]{:S(2)}, u32[]{:S(2)}) collective-permute-start(f32[640,128]{1,0:T(8,128)S(1)} %get-tuple-element.175), channel_id=1, source_target_pairs={{0,8},{4,12},{8,16},{12,20},{16,24},{20,28},{24,0},{28,4},{1,9},{5... | collective-permute-start | bytes 983048 | tf_op jit(solution)/shard_map/while/body/eval_jaxpr/cond/branch_1_fun/ppermute | solution.py:163
  82.0 4.0 %collective-permute-start.13 = (f32[8,128]{1,0:T(8,128)S(1)}, f32[8,128]{1,0:T(8,128)S(1)}, u32[]{:S(2)}, u32[]{:S(2)}) collective-permute-start(f32[8,128]{1,0:T(8,128)S(1)} %maximum_maximum_fusion.1.m0), channel_id=1, source_target_pairs={{0,3},{1,2},{2,1},{3,0},{4,7},{5,6},{6,5},{7,4},{8,11},{9,10},{10,... | collective-permute-start | bytes 12296 | tf_op jit(solution)/shard_map/while/body/eval_jaxpr/cond/branch_1_fun/ppermute | solution.py:167
  87.6 2.0 %collective-permute-done.12.m2 = f32[8,128]{1,0:T(8,128)S(1)} collective-permute-done((f32[8,128]{1,0:T(8,128)S(1)}, f32[8,128]{1,0:T(8,128)S(1)}, u32[]{:S(2)}, u32[]{:S(2)}) %collective-permute-start.12) | collective-permute-done | bytes 4128 | tf_op jit(solution)/shard_map/while/body/eval_jaxpr/cond/branch_1_fun/ppermute | solution.py:167
  89.6 2.3 %branch_1_fun.5 = (f32[1024,128]{1,0:T(8,128)S(1)}, f32[8,128]{1,0:T(8,128)S(1)}) custom-call(f32[8,128]{1,0:T(8,128)S(1)} %maximum_maximum_fusion.1.m0, f32[8,128]{1,0:T(8,128)S(1)} %collective-permute-done.11.m1, f32[8,128]{1,0:T(8,128)S(1)} %collective-permute-done.12.m2, f32[8,128]{1,0:T(8,128)S(1)} %collective-permute-done.13.m3, ...), custom_call_target="tpu_custom_call" | custom-call | flops 3221225472 | tf_op jit(solution)/shard_map/while/body/eval_jaxpr/cond/branch_1_fun/pallas_call | solution.py:151
  92.1 2.0 %branch_1_fun.6 = (f32[128,128]{1,0:T(8,128)S(1)}, f32[512,128]{1,0:T(8,128)S(1)}, f32[136,128]{1,0:T(8,128)S(1)}) custom-call(f32[640,128]{1,0:T(8,128)S(1)} %collective-permute-done.8.early, f32[1024,128]{1,0:T(8,128)S(1)} %get-tuple-element.178.first, f32[8,128]{1,0:T(8,128)S(1)} %get-tuple-element.179.tops), custom_call_target="tpu_custom_call" | custom-call | tf_op jit(solution)/shard_map/while/body/eval_jaxpr/cond/branch_1_fun/pallas_call | solution.py:151
  94.2 3.5 %collective-permute-done.7.late = f32[512,128]{1,0:T(8,128)S(1)} collective-permute-done((f32[512,128]{1,0:T(8,128)S(1)}, f32[512,128]{1,0:T(8,128)S(1)}, u32[]{:S(2)}, u32[]{:S(2)}) %collective-permute-start.7) | collective-permute-done | bytes 262176 | tf_op jit(solution)/shard_map/while/body/eval_jaxpr/cond/branch_1_fun/ppermute | solution.py:163
  98.4 1.2 collective-permute-done.49
  99.7 1.4 %collective-permute-start.50 = (f32[136,128]{1,0:T(8,128)S(1)}, f32[136,128]{1,0:T(8,128)S(1)}, u32[]{:S(2)}, u32[]{:S(2)}) collective-permute-start(f32[136,128]{1,0:T(8,128)S(1)} %add.64.g0), channel_id=1, source_target_pairs={{0,2},{1,3},{2,0},{3,1},{4,6},{5,7},{6,4},{7,5},{8,10},{9,11},{10,... | collective-permute-start | bytes 208904 | tf_op jit(solution)/shard_map/while/body/eval_jaxpr/ppermute | solution.py:167
  104.4 19.3 %conditional.2 = (f32[1024,128]{1,0:T(8,128)S(1)}, f32[1024,128]{1,0:T(8,128)S(1)}, f32[136,128]{1,0:T(8,128)S(1)}, f32[136,128]{1,0:T(8,128)S(1)}, f32[8,128]{1,0:T(8,128)S(1)}) conditional(s32[]{:T(128)} %clamp.7, (f32[128,128]{1,0:T(8,128)S(1)}, f32[1024,128]{1,0:T(8,128)S(1)}, f32[1024,128]{1,0:T(8,128)S(1)}, ...), branch_computations={%region_1.1_spmd, %region_2.2_spmd, %region_3.3_spmd, %region_4.4_... | conditional | flops 3221227520 | bytes 2457920 | solution.py:261
  104.5 2.3 %collective-permute-start.9 = (f32[8,128]{1,0:T(8,128)S(1)}, f32[8,128]{1,0:T(8,128)S(1)}, u32[]{:S(2)}, u32[]{:S(2)}) collective-permute-start(f32[8,128]{1,0:T(8,128)S(1)} %get-tuple-element.176), channel_id=1, source_target_pairs={{0,4},{4,0},{8,12},{12,8},{16,20},{20,16},{24,28},{28,24},{1,13},{... | collective-permute-start | bytes 12296 | tf_op jit(solution)/shard_map/while/body/eval_jaxpr/cond/branch_1_fun/ppermute | solution.py:196
  106.9 1.9 %collective-permute-start.8 = (f32[640,128]{1,0:T(8,128)S(1)}, f32[640,128]{1,0:T(8,128)S(1)}, u32[]{:S(2)}, u32[]{:S(2)}) collective-permute-start(f32[640,128]{1,0:T(8,128)S(1)} %get-tuple-element.175), channel_id=1, source_target_pairs={{0,8},{4,12},{8,16},{12,20},{16,24},{20,28},{24,0},{28,4},{1,9},{5... | collective-permute-start | bytes 983048 | tf_op jit(solution)/shard_map/while/body/eval_jaxpr/cond/branch_1_fun/ppermute | solution.py:163
  108.8 2.5 %collective-permute-start.13 = (f32[8,128]{1,0:T(8,128)S(1)}, f32[8,128]{1,0:T(8,128)S(1)}, u32[]{:S(2)}, u32[]{:S(2)}) collective-permute-start(f32[8,128]{1,0:T(8,128)S(1)} %maximum_maximum_fusion.1.m0), channel_id=1, source_target_pairs={{0,3},{1,2},{2,1},{3,0},{4,7},{5,6},{6,5},{7,4},{8,11},{9,10},{10,... | collective-permute-start | bytes 12296 | tf_op jit(solution)/shard_map/while/body/eval_jaxpr/cond/branch_1_fun/ppermute | solution.py:167
  111.4 0.7 collective-permute-start.12
  112.5 1.6 %collective-permute-start.7 = (f32[512,128]{1,0:T(8,128)S(1)}, f32[512,128]{1,0:T(8,128)S(1)}, u32[]{:S(2)}, u32[]{:S(2)}) collective-permute-start(f32[512,128]{1,0:T(8,128)S(1)} %branch_1_fun.4), channel_id=1, source_target_pairs={{0,8},{4,12},{8,16},{12,20},{16,24},{20,28},{24,0},{28,4},{1,9},{5... | collective-permute-start | bytes 786440 | tf_op jit(solution)/shard_map/while/body/eval_jaxpr/cond/branch_1_fun/ppermute | solution.py:163
  114.1 0.8 collective-permute-done.12.m2
  115.0 2.3 %branch_1_fun.5 = (f32[1024,128]{1,0:T(8,128)S(1)}, f32[8,128]{1,0:T(8,128)S(1)}) custom-call(f32[8,128]{1,0:T(8,128)S(1)} %maximum_maximum_fusion.1.m0, f32[8,128]{1,0:T(8,128)S(1)} %collective-permute-done.11.m1, f32[8,128]{1,0:T(8,128)S(1)} %collective-permute-done.12.m2, f32[8,128]{1,0:T(8,128)S(1)} %collective-permute-done.13.m3, ...), custom_call_target="tpu_custom_call" | custom-call | flops 3221225472 | tf_op jit(solution)/shard_map/while/body/eval_jaxpr/cond/branch_1_fun/pallas_call | solution.py:151
  117.4 2.0 %branch_1_fun.6 = (f32[128,128]{1,0:T(8,128)S(1)}, f32[512,128]{1,0:T(8,128)S(1)}, f32[136,128]{1,0:T(8,128)S(1)}) custom-call(f32[640,128]{1,0:T(8,128)S(1)} %collective-permute-done.8.early, f32[1024,128]{1,0:T(8,128)S(1)} %get-tuple-element.178.first, f32[8,128]{1,0:T(8,128)S(1)} %get-tuple-element.179.tops), custom_call_target="tpu_custom_call" | custom-call | tf_op jit(solution)/shard_map/while/body/eval_jaxpr/cond/branch_1_fun/pallas_call | solution.py:151
  119.4 3.6 %collective-permute-done.7.late = f32[512,128]{1,0:T(8,128)S(1)} collective-permute-done((f32[512,128]{1,0:T(8,128)S(1)}, f32[512,128]{1,0:T(8,128)S(1)}, u32[]{:S(2)}, u32[]{:S(2)}) %collective-permute-start.7) | collective-permute-done | bytes 262176 | tf_op jit(solution)/shard_map/while/body/eval_jaxpr/cond/branch_1_fun/ppermute | solution.py:163
  123.7 1.1 shard_map.51
  (62 shorter events, 10.1 us)
Async XLA Ops:
  0.7 0.7 copy-start
  2.6 11.3 %collective-permute-start.57 = (f32[128,256]{1,0:T(8,128)S(1)}, f32[128,256]{1,0:T(8,128)S(1)}, u32[]{:S(2)}, u32[]{:S(2)}) collective-permute-start(f32[128,256]{1,0:T(8,128)S(1)} %get-tuple-element.303), channel_id=1, source_target_pairs={{0,28},{4,24},{8,20},{12,16},{16,12},{20,8},{24,4},{28,0},{1,29},{... | collective-permute-start | bytes 393224 | tf_op jit(solution)/shard_map/ppermute | solution.py:167
  8.7 15.7 %collective-permute-start.56 = (f32[128,256]{1,0:T(8,128)S(1)}, f32[128,256]{1,0:T(8,128)S(1)}, u32[]{:S(2)}, u32[]{:S(2)}) collective-permute-start(f32[128,256]{1,0:T(8,128)S(1)} %get-tuple-element.304), channel_id=1, source_target_pairs={{0,24},{4,28},{8,16},{12,20},{16,8},{20,12},{24,0},{28,4},{1,25},{... | collective-permute-start | bytes 393224 | tf_op jit(solution)/shard_map/ppermute | solution.py:167
  8.9 20.3 %collective-permute-start.55 = (f32[128,256]{1,0:T(8,128)S(1)}, f32[128,256]{1,0:T(8,128)S(1)}, u32[]{:S(2)}, u32[]{:S(2)}) collective-permute-start(f32[128,256]{1,0:T(8,128)S(1)} %get-tuple-element.305), channel_id=1, source_target_pairs={{0,20},{4,16},{8,28},{12,24},{16,4},{20,0},{24,12},{28,8},{1,21},{... | collective-permute-start | bytes 393224 | tf_op jit(solution)/shard_map/ppermute | solution.py:167
  9.7 21.4 %collective-permute-start.54 = (f32[128,256]{1,0:T(8,128)S(1)}, f32[128,256]{1,0:T(8,128)S(1)}, u32[]{:S(2)}, u32[]{:S(2)}) collective-permute-start(f32[128,256]{1,0:T(8,128)S(1)} %get-tuple-element.306), channel_id=1, source_target_pairs={{0,16},{4,20},{8,24},{12,28},{16,0},{20,4},{24,8},{28,12},{1,17},{... | collective-permute-start | bytes 393224 | tf_op jit(solution)/shard_map/ppermute | solution.py:167
  11.7 19.4 %collective-permute-start.53 = (f32[128,256]{1,0:T(8,128)S(1)}, f32[128,256]{1,0:T(8,128)S(1)}, u32[]{:S(2)}, u32[]{:S(2)}) collective-permute-start(f32[128,256]{1,0:T(8,128)S(1)} %get-tuple-element.307), channel_id=1, source_target_pairs={{0,12},{4,8},{8,4},{12,0},{16,28},{20,24},{24,20},{28,16},{1,13},{... | collective-permute-start | bytes 393224 | tf_op jit(solution)/shard_map/ppermute | solution.py:167
  14.0 18.3 %collective-permute-start.52 = (f32[128,256]{1,0:T(8,128)S(1)}, f32[128,256]{1,0:T(8,128)S(1)}, u32[]{:S(2)}, u32[]{:S(2)}) collective-permute-start(f32[128,256]{1,0:T(8,128)S(1)} %get-tuple-element.308), channel_id=1, source_target_pairs={{0,8},{4,12},{8,0},{12,4},{16,24},{20,28},{24,16},{28,20},{1,9},{5... | collective-permute-start | bytes 393224 | tf_op jit(solution)/shard_map/ppermute | solution.py:167
  24.4 7.8 %collective-permute-start.51 = (f32[128,256]{1,0:T(8,128)S(1)}, f32[128,256]{1,0:T(8,128)S(1)}, u32[]{:S(2)}, u32[]{:S(2)}) collective-permute-start(f32[128,256]{1,0:T(8,128)S(1)} %get-tuple-element.309), channel_id=1, source_target_pairs={{0,4},{4,0},{8,12},{12,8},{16,20},{20,16},{24,28},{28,24},{1,5},{5... | collective-permute-start | bytes 393224 | tf_op jit(solution)/shard_map/ppermute | solution.py:167
  33.3 0.7 copy-start.1
  33.9 1.3 %collective-permute-start.49 = (f32[136,128]{1,0:T(8,128)S(1)}, f32[136,128]{1,0:T(8,128)S(1)}, u32[]{:S(2)}, u32[]{:S(2)}) collective-permute-start(f32[136,128]{1,0:T(8,128)S(1)} %get-tuple-element.414), channel_id=1, source_target_pairs={{0,1},{1,0},{2,3},{3,2},{4,5},{5,4},{6,7},{7,6},{8,9},{9,8},{10,11... | collective-permute-start | bytes 208904 | tf_op jit(solution)/shard_map/while/body/eval_jaxpr/ppermute | solution.py:167
  35.2 4.4 %collective-permute-start.50 = (f32[136,128]{1,0:T(8,128)S(1)}, f32[136,128]{1,0:T(8,128)S(1)}, u32[]{:S(2)}, u32[]{:S(2)}) collective-permute-start(f32[136,128]{1,0:T(8,128)S(1)} %add.64.g0), channel_id=1, source_target_pairs={{0,2},{1,3},{2,0},{3,1},{4,6},{5,7},{6,4},{7,5},{8,10},{9,11},{10,... | collective-permute-start | bytes 208904 | tf_op jit(solution)/shard_map/while/body/eval_jaxpr/ppermute | solution.py:167
  40.0 4.4 %collective-permute-start.31 = (f32[8,128]{1,0:T(8,128)S(1)}, f32[8,128]{1,0:T(8,128)S(1)}, u32[]{:S(2)}, u32[]{:S(2)}) collective-permute-start(f32[8,128]{1,0:T(8,128)S(1)} %get-tuple-element.221), channel_id=1, source_target_pairs={{0,8},{4,12},{8,0},{12,4},{16,24},{20,28},{24,16},{28,20},{1,17},{... | collective-permute-start | bytes 12296 | tf_op jit(solution)/shard_map/while/body/eval_jaxpr/cond/branch_4_fun/ppermute | solution.py:196
  40.1 4.3 %collective-permute-start.30 = (f32[8,128]{1,0:T(8,128)S(1)}, f32[8,128]{1,0:T(8,128)S(1)}, u32[]{:S(2)}, u32[]{:S(2)}) collective-permute-start(f32[8,128]{1,0:T(8,128)S(1)} %get-tuple-element.221), channel_id=1, source_target_pairs={{0,4},{4,0},{8,12},{12,8},{16,20},{20,16},{24,28},{28,24},{1,13},{... | collective-permute-start | bytes 12296 | tf_op jit(solution)/shard_map/while/body/eval_jaxpr/cond/branch_4_fun/ppermute | solution.py:196
  40.8 12.7 %collective-permute-start.29 = (f32[640,128]{1,0:T(8,128)S(1)}, f32[640,128]{1,0:T(8,128)S(1)}, u32[]{:S(2)}, u32[]{:S(2)}) collective-permute-start(f32[640,128]{1,0:T(8,128)S(1)} %get-tuple-element.220), channel_id=1, source_target_pairs={{0,20},{4,24},{8,28},{12,0},{16,4},{20,8},{24,12},{28,16},{1,21},{... | collective-permute-start | bytes 983048 | tf_op jit(solution)/shard_map/while/body/eval_jaxpr/cond/branch_4_fun/ppermute | solution.py:163
  44.4 5.6 %collective-permute-start.34 = (f32[8,128]{1,0:T(8,128)S(1)}, f32[8,128]{1,0:T(8,128)S(1)}, u32[]{:S(2)}, u32[]{:S(2)}) collective-permute-start(f32[8,128]{1,0:T(8,128)S(1)} %maximum_maximum_fusion.4.m0), channel_id=1, source_target_pairs={{0,3},{1,2},{2,1},{3,0},{4,7},{5,6},{6,5},{7,4},{8,11},{9,10},{10,... | collective-permute-start | bytes 12296 | tf_op jit(solution)/shard_map/while/body/eval_jaxpr/cond/branch_4_fun/ppermute | solution.py:167
  47.7 3.6 %collective-permute-start.33 = (f32[8,128]{1,0:T(8,128)S(1)}, f32[8,128]{1,0:T(8,128)S(1)}, u32[]{:S(2)}, u32[]{:S(2)}) collective-permute-start(f32[8,128]{1,0:T(8,128)S(1)} %maximum_maximum_fusion.4.m0), channel_id=1, source_target_pairs={{0,2},{1,3},{2,0},{3,1},{4,6},{5,7},{6,4},{7,5},{8,10},{9,11},{10,... | collective-permute-start | bytes 12296 | tf_op jit(solution)/shard_map/while/body/eval_jaxpr/cond/branch_4_fun/ppermute | solution.py:167
  49.4 1.9 %collective-permute-start.32 = (f32[8,128]{1,0:T(8,128)S(1)}, f32[8,128]{1,0:T(8,128)S(1)}, u32[]{:S(2)}, u32[]{:S(2)}) collective-permute-start(f32[8,128]{1,0:T(8,128)S(1)} %maximum_maximum_fusion.4.m0), channel_id=1, source_target_pairs={{0,1},{1,0},{2,3},{3,2},{4,5},{5,4},{6,7},{7,6},{8,9},{9,8},{10,11... | collective-permute-start | bytes 12296 | tf_op jit(solution)/shard_map/while/body/eval_jaxpr/cond/branch_4_fun/ppermute | solution.py:167
  49.9 9.6 %collective-permute-start.28 = (f32[512,128]{1,0:T(8,128)S(1)}, f32[512,128]{1,0:T(8,128)S(1)}, u32[]{:S(2)}, u32[]{:S(2)}) collective-permute-start(f32[512,128]{1,0:T(8,128)S(1)} %branch_4_fun.4), channel_id=1, source_target_pairs={{0,20},{4,24},{8,28},{12,0},{16,4},{20,8},{24,12},{28,16},{1,21},{... | collective-permute-start | bytes 786440 | tf_op jit(solution)/shard_map/while/body/eval_jaxpr/cond/branch_4_fun/ppermute | solution.py:163
  60.2 1.3 %collective-permute-start.49 = (f32[136,128]{1,0:T(8,128)S(1)}, f32[136,128]{1,0:T(8,128)S(1)}, u32[]{:S(2)}, u32[]{:S(2)}) collective-permute-start(f32[136,128]{1,0:T(8,128)S(1)} %get-tuple-element.414), channel_id=1, source_target_pairs={{0,1},{1,0},{2,3},{3,2},{4,5},{5,4},{6,7},{7,6},{8,9},{9,8},{10,11... | collective-permute-start | bytes 208904 | tf_op jit(solution)/shard_map/while/body/eval_jaxpr/ppermute | solution.py:167
  61.5 4.4 %collective-permute-start.50 = (f32[136,128]{1,0:T(8,128)S(1)}, f32[136,128]{1,0:T(8,128)S(1)}, u32[]{:S(2)}, u32[]{:S(2)}) collective-permute-start(f32[136,128]{1,0:T(8,128)S(1)} %add.64.g0), channel_id=1, source_target_pairs={{0,2},{1,3},{2,0},{3,1},{4,6},{5,7},{6,4},{7,5},{8,10},{9,11},{10,... | collective-permute-start | bytes 208904 | tf_op jit(solution)/shard_map/while/body/eval_jaxpr/ppermute | solution.py:167
  66.3 15.8 %collective-permute-start.10 = (f32[8,128]{1,0:T(8,128)S(1)}, f32[8,128]{1,0:T(8,128)S(1)}, u32[]{:S(2)}, u32[]{:S(2)}) collective-permute-start(f32[8,128]{1,0:T(8,128)S(1)} %get-tuple-element.176), channel_id=1, source_target_pairs={{0,8},{4,12},{8,0},{12,4},{16,24},{20,28},{24,16},{28,20},{1,17},{... | collective-permute-start | bytes 12296 | tf_op jit(solution)/shard_map/while/body/eval_jaxpr/cond/branch_1_fun/ppermute | solution.py:196
  77.0 5.0 %collective-permute-start.9 = (f32[8,128]{1,0:T(8,128)S(1)}, f32[8,128]{1,0:T(8,128)S(1)}, u32[]{:S(2)}, u32[]{:S(2)}) collective-permute-start(f32[8,128]{1,0:T(8,128)S(1)} %get-tuple-element.176), channel_id=1, source_target_pairs={{0,4},{4,0},{8,12},{12,8},{16,20},{20,16},{24,28},{28,24},{1,13},{... | collective-permute-start | bytes 12296 | tf_op jit(solution)/shard_map/while/body/eval_jaxpr/cond/branch_1_fun/ppermute | solution.py:196
  80.1 12.1 %collective-permute-start.8 = (f32[640,128]{1,0:T(8,128)S(1)}, f32[640,128]{1,0:T(8,128)S(1)}, u32[]{:S(2)}, u32[]{:S(2)}) collective-permute-start(f32[640,128]{1,0:T(8,128)S(1)} %get-tuple-element.175), channel_id=1, source_target_pairs={{0,8},{4,12},{8,16},{12,20},{16,24},{20,28},{24,0},{28,4},{1,9},{5... | collective-permute-start | bytes 983048 | tf_op jit(solution)/shard_map/while/body/eval_jaxpr/cond/branch_1_fun/ppermute | solution.py:163
  82.0 5.5 %collective-permute-start.13 = (f32[8,128]{1,0:T(8,128)S(1)}, f32[8,128]{1,0:T(8,128)S(1)}, u32[]{:S(2)}, u32[]{:S(2)}) collective-permute-start(f32[8,128]{1,0:T(8,128)S(1)} %maximum_maximum_fusion.1.m0), channel_id=1, source_target_pairs={{0,3},{1,2},{2,1},{3,0},{4,7},{5,6},{6,5},{7,4},{8,11},{9,10},{10,... | collective-permute-start | bytes 12296 | tf_op jit(solution)/shard_map/while/body/eval_jaxpr/cond/branch_1_fun/ppermute | solution.py:167
  86.0 3.6 %collective-permute-start.12 = (f32[8,128]{1,0:T(8,128)S(1)}, f32[8,128]{1,0:T(8,128)S(1)}, u32[]{:S(2)}, u32[]{:S(2)}) collective-permute-start(f32[8,128]{1,0:T(8,128)S(1)} %maximum_maximum_fusion.1.m0), channel_id=1, source_target_pairs={{0,2},{1,3},{2,0},{3,1},{4,6},{5,7},{6,4},{7,5},{8,10},{9,11},{10,... | collective-permute-start | bytes 12296 | tf_op jit(solution)/shard_map/while/body/eval_jaxpr/cond/branch_1_fun/ppermute | solution.py:167
  86.5 3.1 %collective-permute-start.11 = (f32[8,128]{1,0:T(8,128)S(1)}, f32[8,128]{1,0:T(8,128)S(1)}, u32[]{:S(2)}, u32[]{:S(2)}) collective-permute-start(f32[8,128]{1,0:T(8,128)S(1)} %maximum_maximum_fusion.1.m0), channel_id=1, source_target_pairs={{0,1},{1,0},{2,3},{3,2},{4,5},{5,4},{6,7},{7,6},{8,9},{9,8},{10,11... | collective-permute-start | bytes 12296 | tf_op jit(solution)/shard_map/while/body/eval_jaxpr/cond/branch_1_fun/ppermute | solution.py:167
  87.0 10.7 %collective-permute-start.7 = (f32[512,128]{1,0:T(8,128)S(1)}, f32[512,128]{1,0:T(8,128)S(1)}, u32[]{:S(2)}, u32[]{:S(2)}) collective-permute-start(f32[512,128]{1,0:T(8,128)S(1)} %branch_1_fun.4), channel_id=1, source_target_pairs={{0,8},{4,12},{8,16},{12,20},{16,24},{20,28},{24,0},{28,4},{1,9},{5... | collective-permute-start | bytes 786440 | tf_op jit(solution)/shard_map/while/body/eval_jaxpr/cond/branch_1_fun/ppermute | solution.py:163
  98.4 1.3 %collective-permute-start.49 = (f32[136,128]{1,0:T(8,128)S(1)}, f32[136,128]{1,0:T(8,128)S(1)}, u32[]{:S(2)}, u32[]{:S(2)}) collective-permute-start(f32[136,128]{1,0:T(8,128)S(1)} %get-tuple-element.414), channel_id=1, source_target_pairs={{0,1},{1,0},{2,3},{3,2},{4,5},{5,4},{6,7},{7,6},{8,9},{9,8},{10,11... | collective-permute-start | bytes 208904 | tf_op jit(solution)/shard_map/while/body/eval_jaxpr/ppermute | solution.py:167
  99.7 4.4 %collective-permute-start.50 = (f32[136,128]{1,0:T(8,128)S(1)}, f32[136,128]{1,0:T(8,128)S(1)}, u32[]{:S(2)}, u32[]{:S(2)}) collective-permute-start(f32[136,128]{1,0:T(8,128)S(1)} %add.64.g0), channel_id=1, source_target_pairs={{0,2},{1,3},{2,0},{3,1},{4,6},{5,7},{6,4},{7,5},{8,10},{9,11},{10,... | collective-permute-start | bytes 208904 | tf_op jit(solution)/shard_map/while/body/eval_jaxpr/ppermute | solution.py:167
  104.5 4.3 %collective-permute-start.10 = (f32[8,128]{1,0:T(8,128)S(1)}, f32[8,128]{1,0:T(8,128)S(1)}, u32[]{:S(2)}, u32[]{:S(2)}) collective-permute-start(f32[8,128]{1,0:T(8,128)S(1)} %get-tuple-element.176), channel_id=1, source_target_pairs={{0,8},{4,12},{8,0},{12,4},{16,24},{20,28},{24,16},{28,20},{1,17},{... | collective-permute-start | bytes 12296 | tf_op jit(solution)/shard_map/while/body/eval_jaxpr/cond/branch_1_fun/ppermute | solution.py:196
  104.5 4.3 %collective-permute-start.9 = (f32[8,128]{1,0:T(8,128)S(1)}, f32[8,128]{1,0:T(8,128)S(1)}, u32[]{:S(2)}, u32[]{:S(2)}) collective-permute-start(f32[8,128]{1,0:T(8,128)S(1)} %get-tuple-element.176), channel_id=1, source_target_pairs={{0,4},{4,0},{8,12},{12,8},{16,20},{20,16},{24,28},{28,24},{1,13},{... | collective-permute-start | bytes 12296 | tf_op jit(solution)/shard_map/while/body/eval_jaxpr/cond/branch_1_fun/ppermute | solution.py:196
  106.9 10.5 %collective-permute-start.8 = (f32[640,128]{1,0:T(8,128)S(1)}, f32[640,128]{1,0:T(8,128)S(1)}, u32[]{:S(2)}, u32[]{:S(2)}) collective-permute-start(f32[640,128]{1,0:T(8,128)S(1)} %get-tuple-element.175), channel_id=1, source_target_pairs={{0,8},{4,12},{8,16},{12,20},{16,24},{20,28},{24,0},{28,4},{1,9},{5... | collective-permute-start | bytes 983048 | tf_op jit(solution)/shard_map/while/body/eval_jaxpr/cond/branch_1_fun/ppermute | solution.py:163
  108.8 5.3 %collective-permute-start.13 = (f32[8,128]{1,0:T(8,128)S(1)}, f32[8,128]{1,0:T(8,128)S(1)}, u32[]{:S(2)}, u32[]{:S(2)}) collective-permute-start(f32[8,128]{1,0:T(8,128)S(1)} %maximum_maximum_fusion.1.m0), channel_id=1, source_target_pairs={{0,3},{1,2},{2,1},{3,0},{4,7},{5,6},{6,5},{7,4},{8,11},{9,10},{10,... | collective-permute-start | bytes 12296 | tf_op jit(solution)/shard_map/while/body/eval_jaxpr/cond/branch_1_fun/ppermute | solution.py:167
  111.4 3.6 %collective-permute-start.12 = (f32[8,128]{1,0:T(8,128)S(1)}, f32[8,128]{1,0:T(8,128)S(1)}, u32[]{:S(2)}, u32[]{:S(2)}) collective-permute-start(f32[8,128]{1,0:T(8,128)S(1)} %maximum_maximum_fusion.1.m0), channel_id=1, source_target_pairs={{0,2},{1,3},{2,0},{3,1},{4,6},{5,7},{6,4},{7,5},{8,10},{9,11},{10,... | collective-permute-start | bytes 12296 | tf_op jit(solution)/shard_map/while/body/eval_jaxpr/cond/branch_1_fun/ppermute | solution.py:167
  112.1 2.9 %collective-permute-start.11 = (f32[8,128]{1,0:T(8,128)S(1)}, f32[8,128]{1,0:T(8,128)S(1)}, u32[]{:S(2)}, u32[]{:S(2)}) collective-permute-start(f32[8,128]{1,0:T(8,128)S(1)} %maximum_maximum_fusion.1.m0), channel_id=1, source_target_pairs={{0,1},{1,0},{2,3},{3,2},{4,5},{5,4},{6,7},{7,6},{8,9},{9,8},{10,11... | collective-permute-start | bytes 12296 | tf_op jit(solution)/shard_map/while/body/eval_jaxpr/cond/branch_1_fun/ppermute | solution.py:167
  112.5 10.5 %collective-permute-start.7 = (f32[512,128]{1,0:T(8,128)S(1)}, f32[512,128]{1,0:T(8,128)S(1)}, u32[]{:S(2)}, u32[]{:S(2)}) collective-permute-start(f32[512,128]{1,0:T(8,128)S(1)} %branch_1_fun.4), channel_id=1, source_target_pairs={{0,8},{4,12},{8,16},{12,20},{16,24},{20,28},{24,0},{28,4},{1,9},{5... | collective-permute-start | bytes 786440 | tf_op jit(solution)/shard_map/while/body/eval_jaxpr/cond/branch_1_fun/ppermute | solution.py:163
where the time goes:
time: 126 us; the launch traced here: 125 us
  starting transfers between devices  67.4 us (53%)
  waiting for transfers between devices  26.9 us (21%)
  Pallas kernels  19.1 us (15%)
  loops' own time  6.26 us (5%)
  local copies, waits for them, and re-layouts  3.16 us (3%)
  other arithmetic  1.27 us (1%)
    ppermute x22, starting transfers between devices, swapped(): lax.ppermute(x, axis, [(i, i ^ mask) for i in range(lax.axis_size(axis))])  40.7 us
    pallas_call x17, Pallas kernels, call(): pl.pallas_call(kernel, out_shape=shapes, in_specs=[smem] * smem_in + [vme...  19.1 us
    ppermute x6, starting transfers between devices, most_of_col(): seen.append(lax.ppermute(x, ('col', 'row'), route))  17 us
    ppermute x22, waiting for transfers between devices, swapped(): lax.ppermute(x, axis, [(i, i ^ mask) for i in range(lax.axis_size(axis))])  15.4 us
    ppermute x6, waiting for transfers between devices, forward(): return lax.ppermute(x, 'col', [(i, (i + hop) % n) for i in range(n)])  11.5 us
    ppermute x6, starting transfers between devices, forward(): return lax.ppermute(x, 'col', [(i, (i + hop) % n) for i in range(n)])  9.64 us
    another operation x1, loops' own time, on_device(): lax.scan(one_round, (first, second, gram, tops), partner_shift)  5.99 us
  transfers between devices with their start and end apart: 34, of which 17 were waited for; matrix products, arithmetic and copies ran while one was open for 1% of the time, Pallas kernels for 11%

commit v1 on v0

--- a/solution.py
+++ b/solution.py
@@ -251,7 +251,7 @@
     def joined(first, second, gram, rest, tops):
         return first, second, gram + rest, tops
 
-    def one_round(carry, amount):
+    def one_round(carry, digits):
         first, second, gram, tops = carry
         coupling, measure, early = call(
             functools.partial(couple_kernel, float(total_days)), [(BW, BW), tile, (BW + lead, BW)],
@@ -259,21 +259,23 @@
         )
         branches = [functools.partial(move, hop) for hop in range(lowest, min(n, RADIX))]
         moved = lax.switch(
-            amount % RADIX - lowest, branches, first, second, coupling, measure, early, tops
+            digits[0], branches, first, second, coupling, measure, early, tops
         )
         if len(strides) == 1:
             return joined(*moved), None
         first, early, late, tops = moved
-        for stride in strides[1:]:
+        for digit, stride in zip(digits[1:], strides[1:]):
             routes = [lambda *xs: xs] + [
                 lambda *xs, hop=hop: tuple(forward(x, hop * stride) for x in xs)
                 for hop in range(1, min(RADIX, n // stride))
             ]
-            early, late = lax.switch(amount // stride % RADIX, routes, early, late)
+            early, late = lax.switch(digit, routes, early, late)
         return joined(*settle(early, late, first, tops)), None
 
     tops = jnp.zeros(tile, F32)
-    (first, second, _, tops), _ = lax.scan(one_round, (first, second, gram, tops), partner_shift)
+    digits = [partner_shift // stride % RADIX for stride in strides]
+    digits[0] = digits[0] - lowest
+    (first, second, _, tops), _ = lax.scan(one_round, (first, second, gram, tops), digits)
     return tuple(
         call(last_kernel, [(mine, 2 * BW), (ROUNDS,)], first, second, tops, smem_out=1)
     )

time: 126 us -> 125 us (level); the launches traced: 125 us -> 125 us
  waiting for transfers between devices: 26.9 us -> 39.2 us
  starting transfers between devices: 67.4 us -> 59.9 us
  loops' own time: 6.26 us -> 2.38 us
    ppermute x6, starting transfers between devices: 17 us -> 5.61 us  [most_of_col(): seen.append(lax.ppermute(x, ('col', 'row'), route))]
    ppermute x6, waiting for transfers between devices: 11.5 us -> 21.4 us  [forward(): return lax.ppermute(x, 'col', [(i, (i + hop) % n) for i in range(n)])]
    another operation x4, loops' own time: 6.26 us -> 2.38 us  [the longest x1 2.1 us: on_device(): lax.scan(one_round, (first, second, gram, tops), digits)]
    ppermute x22, starting transfers between devices: 40.7 us -> 43.9 us  [swapped(): lax.ppermute(x, axis, [(i, i ^ mask) for i in range(lax.axis_size(axis))])]
    ppermute x22, waiting for transfers between devices: 15.4 us -> 17.6 us  [swapped(): lax.ppermute(x, axis, [(i, i ^ mask) for i in range(lax.axis_size(axis))])]
  transfers between devices with their start and end apart: 34 -> 34, of which waited for: 17 -> 16; matrix products, arithmetic and copies ran while one was open for 1% -> 1% of each run, Pallas kernels for 11% -> 11%
where the time goes in v1:
time: 125 us
  starting transfers between devices  59.9 us (48%)
  waiting for transfers between devices  39.2 us (31%)
  Pallas kernels  19.1 us (15%)
  local copies, waits for them, and re-layouts  2.52 us (2%)
  loops' own time  2.38 us (2%)
  other arithmetic  1.28 us (1%)
    ppermute x22, starting transfers between devices, swapped(): lax.ppermute(x, axis, [(i, i ^ mask) for i in range(lax.axis_size(axis))])  43.9 us
    ppermute x6, waiting for transfers between devices, forward(): return lax.ppermute(x, 'col', [(i, (i + hop) % n) for i in range(n)])  21.4 us
    pallas_call x17, Pallas kernels, call(): pl.pallas_call(kernel, out_shape=shapes, in_specs=[smem] * smem_in + [vme...  19.1 us
    ppermute x22, waiting for transfers between devices, swapped(): lax.ppermute(x, axis, [(i, i ^ mask) for i in range(lax.axis_size(axis))])  17.6 us
    ppermute x6, starting transfers between devices, forward(): return lax.ppermute(x, 'col', [(i, (i + hop) % n) for i in range(n)])  10.4 us
    ppermute x6, starting transfers between devices, most_of_col(): seen.append(lax.ppermute(x, ('col', 'row'), route))  5.61 us
  transfers between devices with their start and end apart: 34, of which 16 were waited for; matrix products, arithmetic and copies ran while one was open for 1% of the time, Pallas kernels for 11%

profile of v1, /device:TPU:0, one launch (start us, length us, event | category | flops | bytes accessed | tf_op | source)
XLA Modules:
  0.0 125.1 jit_solution(1059339150396217716)
XLA Ops:
  1.3 1.2 convert_multiply_fusion
  2.6 6.0 %collective-permute-start.57 = (f32[128,256]{1,0:T(8,128)S(1)}, f32[128,256]{1,0:T(8,128)S(1)}, u32[]{:S(2)}, u32[]{:S(2)}) collective-permute-start(f32[128,256]{1,0:T(8,128)S(1)} %get-tuple-element.254), channel_id=1, source_target_pairs={{0,28},{4,24},{8,20},{12,16},{16,12},{20,8},{24,4},{28,0},{1,29},{... | collective-permute-start | bytes 393224 | tf_op jit(solution)/shard_map/ppermute | solution.py:167
  9.7 2.0 %collective-permute-start.54 = (f32[128,256]{1,0:T(8,128)S(1)}, f32[128,256]{1,0:T(8,128)S(1)}, u32[]{:S(2)}, u32[]{:S(2)}) collective-permute-start(f32[128,256]{1,0:T(8,128)S(1)} %get-tuple-element.257), channel_id=1, source_target_pairs={{0,16},{4,20},{8,24},{12,28},{16,0},{20,4},{24,8},{28,12},{1,17},{... | collective-permute-start | bytes 393224 | tf_op jit(solution)/shard_map/ppermute | solution.py:167
  11.7 2.3 %collective-permute-start.53 = (f32[128,256]{1,0:T(8,128)S(1)}, f32[128,256]{1,0:T(8,128)S(1)}, u32[]{:S(2)}, u32[]{:S(2)}) collective-permute-start(f32[128,256]{1,0:T(8,128)S(1)} %get-tuple-element.258), channel_id=1, source_target_pairs={{0,12},{4,8},{8,4},{12,0},{16,28},{20,24},{24,20},{28,16},{1,13},{... | collective-permute-start | bytes 393224 | tf_op jit(solution)/shard_map/ppermute | solution.py:167
  14.0 10.4 %collective-permute-start.52 = (f32[128,256]{1,0:T(8,128)S(1)}, f32[128,256]{1,0:T(8,128)S(1)}, u32[]{:S(2)}, u32[]{:S(2)}) collective-permute-start(f32[128,256]{1,0:T(8,128)S(1)} %get-tuple-element.259), channel_id=1, source_target_pairs={{0,8},{4,12},{8,0},{12,4},{16,24},{20,28},{24,16},{28,20},{1,9},{5... | collective-permute-start | bytes 393224 | tf_op jit(solution)/shard_map/ppermute | solution.py:167
  24.4 1.4 %collective-permute-start.51 = (f32[128,256]{1,0:T(8,128)S(1)}, f32[128,256]{1,0:T(8,128)S(1)}, u32[]{:S(2)}, u32[]{:S(2)}) collective-permute-start(f32[128,256]{1,0:T(8,128)S(1)} %get-tuple-element.260), channel_id=1, source_target_pairs={{0,4},{4,0},{8,12},{12,8},{16,20},{20,16},{24,28},{28,24},{1,5},{5... | collective-permute-start | bytes 393224 | tf_op jit(solution)/shard_map/ppermute | solution.py:167
  25.8 3.5 %collective-permute-done.55.refs_5_ = f32[128,256]{1,0:T(8,128)S(1)} collective-permute-done((f32[128,256]{1,0:T(8,128)S(1)}, f32[128,256]{1,0:T(8,128)S(1)}, u32[]{:S(2)}, u32[]{:S(2)}) %collective-permute-start.55) | collective-permute-done | bytes 131104 | tf_op jit(solution)/shard_map/ppermute | solution.py:167
  29.2 1.9 %collective-permute-done.54.refs_4_ = f32[128,256]{1,0:T(8,128)S(1)} collective-permute-done((f32[128,256]{1,0:T(8,128)S(1)}, f32[128,256]{1,0:T(8,128)S(1)}, u32[]{:S(2)}, u32[]{:S(2)}) %collective-permute-start.54) | collective-permute-done | bytes 131104 | tf_op jit(solution)/shard_map/ppermute | solution.py:167
  31.1 1.1 collective-permute-done.52.refs_2_
  32.2 1.1 shard_map.50
  33.3 90.7 %while.16 = (s32[]{:T(128)}, f32[1024,128]{1,0:T(8,128)S(1)}, f32[1024,128]{1,0:T(8,128)S(1)}, f32[136,128]{1,0:T(8,128)S(1)}, f32[8,128]{1,0:T(8,128)S(1)}, /*i...) while((s32[]{:T(128)}, f32[1024,128]{1,0:T(8,128)S(1)}, f32[1024,128]{1,0:T(8,128)S(1)}, ...), condition=%wide.region_8.9_spmd, body=%wide.region_0.8_spmd.sunk | while | flops 3221262336 | bytes 3433025 | solution.py:278
  33.4 1.2 collective-permute-done.49
  34.7 1.6 %collective-permute-start.50 = (f32[136,128]{1,0:T(8,128)S(1)}, f32[136,128]{1,0:T(8,128)S(1)}, u32[]{:S(2)}, u32[]{:S(2)}) collective-permute-start(f32[136,128]{1,0:T(8,128)S(1)} %add.57.g0), channel_id=1, source_target_pairs={{0,2},{1,3},{2,0},{3,1},{4,6},{5,7},{6,4},{7,5},{8,10},{9,11},{10,... | collective-permute-start | bytes 208904 | tf_op jit(solution)/shard_map/while/body/eval_jaxpr/ppermute | solution.py:167
  37.5 1.6 %collective-permute-done.50.g1 = f32[136,128]{1,0:T(8,128)S(1)} collective-permute-done((f32[136,128]{1,0:T(8,128)S(1)}, f32[136,128]{1,0:T(8,128)S(1)}, u32[]{:S(2)}, u32[]{:S(2)}) %collective-permute-start.50) | collective-permute-done | bytes 69664 | tf_op jit(solution)/shard_map/while/body/eval_jaxpr/ppermute | solution.py:167
  39.4 19.3 %conditional.2 = (f32[1024,128]{1,0:T(8,128)S(1)}, f32[1024,128]{1,0:T(8,128)S(1)}, f32[136,128]{1,0:T(8,128)S(1)}, f32[136,128]{1,0:T(8,128)S(1)}, f32[8,128]{1,0:T(8,128)S(1)}) conditional(s32[]{:T(128)} %bitcast.2, (f32[128,128]{1,0:T(8,128)S(1)}, f32[1024,128]{1,0:T(8,128)S(1)}, f32[1024,128]{1,0:T(8,128)S(1)}, ...), branch_computations={%region_1.1_spmd, %region_2.2_spmd, %region_3.3_spmd, %region_4.4_... | conditional | flops 3221227520 | bytes 2457920 | solution.py:261
  39.5 0.8 collective-permute-start.44
  40.3 3.0 %collective-permute-start.43 = (f32[640,128]{1,0:T(8,128)S(1)}, f32[640,128]{1,0:T(8,128)S(1)}, u32[]{:S(2)}, u32[]{:S(2)}) collective-permute-start(f32[640,128]{1,0:T(8,128)S(1)} %get-tuple-element.201), channel_id=1, source_target_pairs={{0,28},{4,0},{8,4},{12,8},{16,12},{20,16},{24,20},{28,24},{1,29},{... | collective-permute-start | bytes 983048 | tf_op jit(solution)/shard_map/while/body/eval_jaxpr/cond/branch_6_fun/ppermute | solution.py:163
  43.3 3.9 %collective-permute-start.48 = (f32[8,128]{1,0:T(8,128)S(1)}, f32[8,128]{1,0:T(8,128)S(1)}, u32[]{:S(2)}, u32[]{:S(2)}) collective-permute-start(f32[8,128]{1,0:T(8,128)S(1)} %maximum_maximum_fusion.6.m0), channel_id=1, source_target_pairs={{0,3},{1,2},{2,1},{3,0},{4,7},{5,6},{6,5},{7,4},{8,11},{9,10},{10,... | collective-permute-start | bytes 12296 | tf_op jit(solution)/shard_map/while/body/eval_jaxpr/cond/branch_6_fun/ppermute | solution.py:167
  47.2 1.6 %collective-permute-start.47 = (f32[8,128]{1,0:T(8,128)S(1)}, f32[8,128]{1,0:T(8,128)S(1)}, u32[]{:S(2)}, u32[]{:S(2)}) collective-permute-start(f32[8,128]{1,0:T(8,128)S(1)} %maximum_maximum_fusion.6.m0), channel_id=1, source_target_pairs={{0,2},{1,3},{2,0},{3,1},{4,6},{5,7},{6,4},{7,5},{8,10},{9,11},{10,... | collective-permute-start | bytes 12296 | tf_op jit(solution)/shard_map/while/body/eval_jaxpr/cond/branch_6_fun/ppermute | solution.py:167
  49.4 1.6 %collective-permute-start.42 = (f32[512,128]{1,0:T(8,128)S(1)}, f32[512,128]{1,0:T(8,128)S(1)}, u32[]{:S(2)}, u32[]{:S(2)}) collective-permute-start(f32[512,128]{1,0:T(8,128)S(1)} %branch_6_fun.4), channel_id=1, source_target_pairs={{0,28},{4,0},{8,4},{12,8},{16,12},{20,16},{24,20},{28,24},{1,29},{... | collective-permute-start | bytes 786440 | tf_op jit(solution)/shard_map/while/body/eval_jaxpr/cond/branch_6_fun/ppermute | solution.py:163
  51.0 2.3 %branch_6_fun.5 = (f32[1024,128]{1,0:T(8,128)S(1)}, f32[8,128]{1,0:T(8,128)S(1)}) custom-call(f32[8,128]{1,0:T(8,128)S(1)} %maximum_maximum_fusion.6.m0, f32[8,128]{1,0:T(8,128)S(1)} %collective-permute-done.46.m1, f32[8,128]{1,0:T(8,128)S(1)} %collective-permute-done.47.m2, f32[8,128]{1,0:T(8,128)S(1)} %collective-permute-done.48.m3, ...), custom_call_target="tpu_custom_call" | custom-call | flops 3221225472 | tf_op jit(solution)/shard_map/while/body/eval_jaxpr/cond/branch_6_fun/pallas_call | solution.py:151
  53.3 2.0 %branch_6_fun.6 = (f32[128,128]{1,0:T(8,128)S(1)}, f32[512,128]{1,0:T(8,128)S(1)}, f32[136,128]{1,0:T(8,128)S(1)}) custom-call(f32[640,128]{1,0:T(8,128)S(1)} %collective-permute-done.43.early, f32[1024,128]{1,0:T(8,128)S(1)} %get-tuple-element.204.first, f32[8,128]{1,0:T(8,128)S(1)} %get-tuple-element.205.tops), custom_call_target="tpu_custom_call" | custom-call | tf_op jit(solution)/shard_map/while/body/eval_jaxpr/cond/branch_6_fun/pallas_call | solution.py:151
  55.3 2.7 %collective-permute-done.42.late = f32[512,128]{1,0:T(8,128)S(1)} collective-permute-done((f32[512,128]{1,0:T(8,128)S(1)}, f32[512,128]{1,0:T(8,128)S(1)}, u32[]{:S(2)}, u32[]{:S(2)}) %collective-permute-start.42) | collective-permute-done | bytes 262176 | tf_op jit(solution)/shard_map/while/body/eval_jaxpr/cond/branch_6_fun/ppermute | solution.py:163
  58.8 1.2 collective-permute-done.49
  60.1 1.5 %collective-permute-start.50 = (f32[136,128]{1,0:T(8,128)S(1)}, f32[136,128]{1,0:T(8,128)S(1)}, u32[]{:S(2)}, u32[]{:S(2)}) collective-permute-start(f32[136,128]{1,0:T(8,128)S(1)} %add.57.g0), channel_id=1, source_target_pairs={{0,2},{1,3},{2,0},{3,1},{4,6},{5,7},{6,4},{7,5},{8,10},{9,11},{10,... | collective-permute-start | bytes 208904 | tf_op jit(solution)/shard_map/while/body/eval_jaxpr/ppermute | solution.py:167
  62.8 1.6 %collective-permute-done.50.g1 = f32[136,128]{1,0:T(8,128)S(1)} collective-permute-done((f32[136,128]{1,0:T(8,128)S(1)}, f32[136,128]{1,0:T(8,128)S(1)}, u32[]{:S(2)}, u32[]{:S(2)}) %collective-permute-start.50) | collective-permute-done | bytes 69664 | tf_op jit(solution)/shard_map/while/body/eval_jaxpr/ppermute | solution.py:167
  64.8 21.7 %conditional.2 = (f32[1024,128]{1,0:T(8,128)S(1)}, f32[1024,128]{1,0:T(8,128)S(1)}, f32[136,128]{1,0:T(8,128)S(1)}, f32[136,128]{1,0:T(8,128)S(1)}, f32[8,128]{1,0:T(8,128)S(1)}) conditional(s32[]{:T(128)} %bitcast.2, (f32[128,128]{1,0:T(8,128)S(1)}, f32[1024,128]{1,0:T(8,128)S(1)}, f32[1024,128]{1,0:T(8,128)S(1)}, ...), branch_computations={%region_1.1_spmd, %region_2.2_spmd, %region_3.3_spmd, %region_4.4_... | conditional | flops 3221227520 | bytes 2457920 | solution.py:261
  64.9 1.9 %collective-permute-start.9 = (f32[8,128]{1,0:T(8,128)S(1)}, f32[8,128]{1,0:T(8,128)S(1)}, u32[]{:S(2)}, u32[]{:S(2)}) collective-permute-start(f32[8,128]{1,0:T(8,128)S(1)} %get-tuple-element.127), channel_id=1, source_target_pairs={{0,4},{4,0},{8,12},{12,8},{16,20},{20,16},{24,28},{28,24},{1,13},{... | collective-permute-start | bytes 12296 | tf_op jit(solution)/shard_map/while/body/eval_jaxpr/cond/branch_1_fun/ppermute | solution.py:196
  66.8 1.9 %collective-permute-start.8 = (f32[640,128]{1,0:T(8,128)S(1)}, f32[640,128]{1,0:T(8,128)S(1)}, u32[]{:S(2)}, u32[]{:S(2)}) collective-permute-start(f32[640,128]{1,0:T(8,128)S(1)} %get-tuple-element.126), channel_id=1, source_target_pairs={{0,8},{4,12},{8,16},{12,20},{16,24},{20,28},{24,0},{28,4},{1,9},{5... | collective-permute-start | bytes 983048 | tf_op jit(solution)/shard_map/while/body/eval_jaxpr/cond/branch_1_fun/ppermute | solution.py:163
  68.7 6.2 %collective-permute-start.13 = (f32[8,128]{1,0:T(8,128)S(1)}, f32[8,128]{1,0:T(8,128)S(1)}, u32[]{:S(2)}, u32[]{:S(2)}) collective-permute-start(f32[8,128]{1,0:T(8,128)S(1)} %maximum_maximum_fusion.1.m0), channel_id=1, source_target_pairs={{0,3},{1,2},{2,1},{3,0},{4,7},{5,6},{6,5},{7,4},{8,11},{9,10},{10,... | collective-permute-start | bytes 12296 | tf_op jit(solution)/shard_map/while/body/eval_jaxpr/cond/branch_1_fun/ppermute | solution.py:167
  76.3 2.3 %collective-permute-done.12.m2 = f32[8,128]{1,0:T(8,128)S(1)} collective-permute-done((f32[8,128]{1,0:T(8,128)S(1)}, f32[8,128]{1,0:T(8,128)S(1)}, u32[]{:S(2)}, u32[]{:S(2)}) %collective-permute-start.12) | collective-permute-done | bytes 4128 | tf_op jit(solution)/shard_map/while/body/eval_jaxpr/cond/branch_1_fun/ppermute | solution.py:167
  78.5 2.3 %branch_1_fun.5 = (f32[1024,128]{1,0:T(8,128)S(1)}, f32[8,128]{1,0:T(8,128)S(1)}) custom-call(f32[8,128]{1,0:T(8,128)S(1)} %maximum_maximum_fusion.1.m0, f32[8,128]{1,0:T(8,128)S(1)} %collective-permute-done.11.m1, f32[8,128]{1,0:T(8,128)S(1)} %collective-permute-done.12.m2, f32[8,128]{1,0:T(8,128)S(1)} %collective-permute-done.13.m3, ...), custom_call_target="tpu_custom_call" | custom-call | flops 3221225472 | tf_op jit(solution)/shard_map/while/body/eval_jaxpr/cond/branch_1_fun/pallas_call | solution.py:151
  80.8 2.0 %branch_1_fun.6 = (f32[128,128]{1,0:T(8,128)S(1)}, f32[512,128]{1,0:T(8,128)S(1)}, f32[136,128]{1,0:T(8,128)S(1)}) custom-call(f32[640,128]{1,0:T(8,128)S(1)} %collective-permute-done.8.early, f32[1024,128]{1,0:T(8,128)S(1)} %get-tuple-element.129.first, f32[8,128]{1,0:T(8,128)S(1)} %get-tuple-element.130.tops), custom_call_target="tpu_custom_call" | custom-call | tf_op jit(solution)/shard_map/while/body/eval_jaxpr/cond/branch_1_fun/pallas_call | solution.py:151
  82.8 3.1 %collective-permute-done.7.late = f32[512,128]{1,0:T(8,128)S(1)} collective-permute-done((f32[512,128]{1,0:T(8,128)S(1)}, f32[512,128]{1,0:T(8,128)S(1)}, u32[]{:S(2)}, u32[]{:S(2)}) %collective-permute-start.7) | collective-permute-done | bytes 262176 | tf_op jit(solution)/shard_map/while/body/eval_jaxpr/cond/branch_1_fun/ppermute | solution.py:163
  86.7 1.2 collective-permute-done.49
  87.9 2.1 %collective-permute-start.50 = (f32[136,128]{1,0:T(8,128)S(1)}, f32[136,128]{1,0:T(8,128)S(1)}, u32[]{:S(2)}, u32[]{:S(2)}) collective-permute-start(f32[136,128]{1,0:T(8,128)S(1)} %add.57.g0), channel_id=1, source_target_pairs={{0,2},{1,3},{2,0},{3,1},{4,6},{5,7},{6,4},{7,5},{8,10},{9,11},{10,... | collective-permute-start | bytes 208904 | tf_op jit(solution)/shard_map/while/body/eval_jaxpr/ppermute | solution.py:167
  91.3 1.3 %collective-permute-done.50.g1 = f32[136,128]{1,0:T(8,128)S(1)} collective-permute-done((f32[136,128]{1,0:T(8,128)S(1)}, f32[136,128]{1,0:T(8,128)S(1)}, u32[]{:S(2)}, u32[]{:S(2)}) %collective-permute-start.50) | collective-permute-done | bytes 69664 | tf_op jit(solution)/shard_map/while/body/eval_jaxpr/ppermute | solution.py:167
  92.9 31.1 %conditional.2 = (f32[1024,128]{1,0:T(8,128)S(1)}, f32[1024,128]{1,0:T(8,128)S(1)}, f32[136,128]{1,0:T(8,128)S(1)}, f32[136,128]{1,0:T(8,128)S(1)}, f32[8,128]{1,0:T(8,128)S(1)}) conditional(s32[]{:T(128)} %bitcast.2, (f32[128,128]{1,0:T(8,128)S(1)}, f32[1024,128]{1,0:T(8,128)S(1)}, f32[1024,128]{1,0:T(8,128)S(1)}, ...), branch_computations={%region_1.1_spmd, %region_2.2_spmd, %region_3.3_spmd, %region_4.4_... | conditional | flops 3221227520 | bytes 2457920 | solution.py:261
  93.0 2.8 %collective-permute-start.16 = (f32[8,128]{1,0:T(8,128)S(1)}, f32[8,128]{1,0:T(8,128)S(1)}, u32[]{:S(2)}, u32[]{:S(2)}) collective-permute-start(f32[8,128]{1,0:T(8,128)S(1)} %get-tuple-element.142), channel_id=1, source_target_pairs={{0,4},{4,0},{8,12},{12,8},{16,20},{20,16},{24,28},{28,24},{1,13},{... | collective-permute-start | bytes 12296 | tf_op jit(solution)/shard_map/while/body/eval_jaxpr/cond/branch_2_fun/ppermute | solution.py:196
  95.8 1.4 %collective-permute-start.15 = (f32[640,128]{1,0:T(8,128)S(1)}, f32[640,128]{1,0:T(8,128)S(1)}, u32[]{:S(2)}, u32[]{:S(2)}) collective-permute-start(f32[640,128]{1,0:T(8,128)S(1)} %get-tuple-element.141), channel_id=1, source_target_pairs={{0,12},{4,16},{8,20},{12,24},{16,28},{20,0},{24,4},{28,8},{1,13},{... | collective-permute-start | bytes 983048 | tf_op jit(solution)/shard_map/while/body/eval_jaxpr/cond/branch_2_fun/ppermute | solution.py:163
  97.4 2.1 %collective-permute-start.20 = (f32[8,128]{1,0:T(8,128)S(1)}, f32[8,128]{1,0:T(8,128)S(1)}, u32[]{:S(2)}, u32[]{:S(2)}) collective-permute-start(f32[8,128]{1,0:T(8,128)S(1)} %maximum_maximum_fusion.2.m0), channel_id=1, source_target_pairs={{0,3},{1,2},{2,1},{3,0},{4,7},{5,6},{6,5},{7,4},{8,11},{9,10},{10,... | collective-permute-start | bytes 12296 | tf_op jit(solution)/shard_map/while/body/eval_jaxpr/cond/branch_2_fun/ppermute | solution.py:167
  99.5 1.2 collective-permute-start.19
  101.2 2.3 %collective-permute-start.14 = (f32[512,128]{1,0:T(8,128)S(1)}, f32[512,128]{1,0:T(8,128)S(1)}, u32[]{:S(2)}, u32[]{:S(2)}) collective-permute-start(f32[512,128]{1,0:T(8,128)S(1)} %branch_2_fun.4), channel_id=1, source_target_pairs={{0,12},{4,16},{8,20},{12,24},{16,28},{20,0},{24,4},{28,8},{1,13},{... | collective-permute-start | bytes 786440 | tf_op jit(solution)/shard_map/while/body/eval_jaxpr/cond/branch_2_fun/ppermute | solution.py:163
  103.5 2.3 %branch_2_fun.5 = (f32[1024,128]{1,0:T(8,128)S(1)}, f32[8,128]{1,0:T(8,128)S(1)}) custom-call(f32[8,128]{1,0:T(8,128)S(1)} %maximum_maximum_fusion.2.m0, f32[8,128]{1,0:T(8,128)S(1)} %collective-permute-done.18.m1, f32[8,128]{1,0:T(8,128)S(1)} %collective-permute-done.19.m2, f32[8,128]{1,0:T(8,128)S(1)} %collective-permute-done.20.m3, ...), custom_call_target="tpu_custom_call" | custom-call | flops 3221225472 | tf_op jit(solution)/shard_map/while/body/eval_jaxpr/cond/branch_2_fun/pallas_call | solution.py:151
  105.8 13.8 %collective-permute-done.15.early = f32[640,128]{1,0:T(8,128)S(1)} collective-permute-done((f32[640,128]{1,0:T(8,128)S(1)}, f32[640,128]{1,0:T(8,128)S(1)}, u32[]{:S(2)}, u32[]{:S(2)}) %collective-permute-start.15) | collective-permute-done | bytes 327712 | tf_op jit(solution)/shard_map/while/body/eval_jaxpr/cond/branch_2_fun/ppermute | solution.py:163
  119.6 2.0 %branch_2_fun.6 = (f32[128,128]{1,0:T(8,128)S(1)}, f32[512,128]{1,0:T(8,128)S(1)}, f32[136,128]{1,0:T(8,128)S(1)}) custom-call(f32[640,128]{1,0:T(8,128)S(1)} %collective-permute-done.15.early, f32[1024,128]{1,0:T(8,128)S(1)} %get-tuple-element.144.first, f32[8,128]{1,0:T(8,128)S(1)} %get-tuple-element.145.tops), custom_call_target="tpu_custom_call" | custom-call | tf_op jit(solution)/shard_map/while/body/eval_jaxpr/cond/branch_2_fun/pallas_call | solution.py:151
  121.7 1.7 %collective-permute-done.14.late = f32[512,128]{1,0:T(8,128)S(1)} collective-permute-done((f32[512,128]{1,0:T(8,128)S(1)}, f32[512,128]{1,0:T(8,128)S(1)}, u32[]{:S(2)}, u32[]{:S(2)}) %collective-permute-start.14) | collective-permute-done | bytes 262176 | tf_op jit(solution)/shard_map/while/body/eval_jaxpr/cond/branch_2_fun/ppermute | solution.py:163
  124.0 1.1 shard_map.51
  (63 shorter events, 9.5 us)
Async XLA Ops:
  0.7 0.7 copy-start
  2.6 11.3 %collective-permute-start.57 = (f32[128,256]{1,0:T(8,128)S(1)}, f32[128,256]{1,0:T(8,128)S(1)}, u32[]{:S(2)}, u32[]{:S(2)}) collective-permute-start(f32[128,256]{1,0:T(8,128)S(1)} %get-tuple-element.254), channel_id=1, source_target_pairs={{0,28},{4,24},{8,20},{12,16},{16,12},{20,8},{24,4},{28,0},{1,29},{... | collective-permute-start | bytes 393224 | tf_op jit(solution)/shard_map/ppermute | solution.py:167
  8.7 15.7 %collective-permute-start.56 = (f32[128,256]{1,0:T(8,128)S(1)}, f32[128,256]{1,0:T(8,128)S(1)}, u32[]{:S(2)}, u32[]{:S(2)}) collective-permute-start(f32[128,256]{1,0:T(8,128)S(1)} %get-tuple-element.255), channel_id=1, source_target_pairs={{0,24},{4,28},{8,16},{12,20},{16,8},{20,12},{24,0},{28,4},{1,25},{... | collective-permute-start | bytes 393224 | tf_op jit(solution)/shard_map/ppermute | solution.py:167
  8.9 20.3 %collective-permute-start.55 = (f32[128,256]{1,0:T(8,128)S(1)}, f32[128,256]{1,0:T(8,128)S(1)}, u32[]{:S(2)}, u32[]{:S(2)}) collective-permute-start(f32[128,256]{1,0:T(8,128)S(1)} %get-tuple-element.256), channel_id=1, source_target_pairs={{0,20},{4,16},{8,28},{12,24},{16,4},{20,0},{24,12},{28,8},{1,21},{... | collective-permute-start | bytes 393224 | tf_op jit(solution)/shard_map/ppermute | solution.py:167
  9.7 21.4 %collective-permute-start.54 = (f32[128,256]{1,0:T(8,128)S(1)}, f32[128,256]{1,0:T(8,128)S(1)}, u32[]{:S(2)}, u32[]{:S(2)}) collective-permute-start(f32[128,256]{1,0:T(8,128)S(1)} %get-tuple-element.257), channel_id=1, source_target_pairs={{0,16},{4,20},{8,24},{12,28},{16,0},{20,4},{24,8},{28,12},{1,17},{... | collective-permute-start | bytes 393224 | tf_op jit(solution)/shard_map/ppermute | solution.py:167
  11.7 19.4 %collective-permute-start.53 = (f32[128,256]{1,0:T(8,128)S(1)}, f32[128,256]{1,0:T(8,128)S(1)}, u32[]{:S(2)}, u32[]{:S(2)}) collective-permute-start(f32[128,256]{1,0:T(8,128)S(1)} %get-tuple-element.258), channel_id=1, source_target_pairs={{0,12},{4,8},{8,4},{12,0},{16,28},{20,24},{24,20},{28,16},{1,13},{... | collective-permute-start | bytes 393224 | tf_op jit(solution)/shard_map/ppermute | solution.py:167
  14.0 11.8 %copy-start.1 = (s32[3]{0:T(128)S(1)}, s32[3]{0:T(128)}, u32[]{:S(2)}) copy-start(s32[3]{0:T(128)} %param.14) | copy-start | bytes 40
  14.0 18.3 %collective-permute-start.52 = (f32[128,256]{1,0:T(8,128)S(1)}, f32[128,256]{1,0:T(8,128)S(1)}, u32[]{:S(2)}, u32[]{:S(2)}) collective-permute-start(f32[128,256]{1,0:T(8,128)S(1)} %get-tuple-element.259), channel_id=1, source_target_pairs={{0,8},{4,12},{8,0},{12,4},{16,24},{20,28},{24,16},{28,20},{1,9},{5... | collective-permute-start | bytes 393224 | tf_op jit(solution)/shard_map/ppermute | solution.py:167
  24.4 7.8 %collective-permute-start.51 = (f32[128,256]{1,0:T(8,128)S(1)}, f32[128,256]{1,0:T(8,128)S(1)}, u32[]{:S(2)}, u32[]{:S(2)}) collective-permute-start(f32[128,256]{1,0:T(8,128)S(1)} %get-tuple-element.260), channel_id=1, source_target_pairs={{0,4},{4,0},{8,12},{12,8},{16,20},{20,16},{24,28},{28,24},{1,5},{5... | collective-permute-start | bytes 393224 | tf_op jit(solution)/shard_map/ppermute | solution.py:167
  33.3 1.3 %collective-permute-start.49 = (f32[136,128]{1,0:T(8,128)S(1)}, f32[136,128]{1,0:T(8,128)S(1)}, u32[]{:S(2)}, u32[]{:S(2)}) collective-permute-start(f32[136,128]{1,0:T(8,128)S(1)} %get-tuple-element.362), channel_id=1, source_target_pairs={{0,1},{1,0},{2,3},{3,2},{4,5},{5,4},{6,7},{7,6},{8,9},{9,8},{10,11... | collective-permute-start | bytes 208904 | tf_op jit(solution)/shard_map/while/body/eval_jaxpr/ppermute | solution.py:167
  34.7 4.4 %collective-permute-start.50 = (f32[136,128]{1,0:T(8,128)S(1)}, f32[136,128]{1,0:T(8,128)S(1)}, u32[]{:S(2)}, u32[]{:S(2)}) collective-permute-start(f32[136,128]{1,0:T(8,128)S(1)} %add.57.g0), channel_id=1, source_target_pairs={{0,2},{1,3},{2,0},{3,1},{4,6},{5,7},{6,4},{7,5},{8,10},{9,11},{10,... | collective-permute-start | bytes 208904 | tf_op jit(solution)/shard_map/while/body/eval_jaxpr/ppermute | solution.py:167
  39.5 3.9 %collective-permute-start.45 = (f32[8,128]{1,0:T(8,128)S(1)}, f32[8,128]{1,0:T(8,128)S(1)}, u32[]{:S(2)}, u32[]{:S(2)}) collective-permute-start(f32[8,128]{1,0:T(8,128)S(1)} %get-tuple-element.202), channel_id=1, source_target_pairs={{0,8},{4,12},{8,0},{12,4},{16,24},{20,28},{24,16},{28,20},{1,17},{... | collective-permute-start | bytes 12296 | tf_op jit(solution)/shard_map/while/body/eval_jaxpr/cond/branch_6_fun/ppermute | solution.py:196
  39.5 3.8 %collective-permute-start.44 = (f32[8,128]{1,0:T(8,128)S(1)}, f32[8,128]{1,0:T(8,128)S(1)}, u32[]{:S(2)}, u32[]{:S(2)}) collective-permute-start(f32[8,128]{1,0:T(8,128)S(1)} %get-tuple-element.202), channel_id=1, source_target_pairs={{0,4},{4,0},{8,12},{12,8},{16,20},{20,16},{24,28},{28,24},{1,13},{... | collective-permute-start | bytes 12296 | tf_op jit(solution)/shard_map/while/body/eval_jaxpr/cond/branch_6_fun/ppermute | solution.py:196
  40.3 13.0 %collective-permute-start.43 = (f32[640,128]{1,0:T(8,128)S(1)}, f32[640,128]{1,0:T(8,128)S(1)}, u32[]{:S(2)}, u32[]{:S(2)}) collective-permute-start(f32[640,128]{1,0:T(8,128)S(1)} %get-tuple-element.201), channel_id=1, source_target_pairs={{0,28},{4,0},{8,4},{12,8},{16,12},{20,16},{24,20},{28,24},{1,29},{... | collective-permute-start | bytes 983048 | tf_op jit(solution)/shard_map/while/body/eval_jaxpr/cond/branch_6_fun/ppermute | solution.py:163
  43.3 7.6 %collective-permute-start.48 = (f32[8,128]{1,0:T(8,128)S(1)}, f32[8,128]{1,0:T(8,128)S(1)}, u32[]{:S(2)}, u32[]{:S(2)}) collective-permute-start(f32[8,128]{1,0:T(8,128)S(1)} %maximum_maximum_fusion.6.m0), channel_id=1, source_target_pairs={{0,3},{1,2},{2,1},{3,0},{4,7},{5,6},{6,5},{7,4},{8,11},{9,10},{10,... | collective-permute-start | bytes 12296 | tf_op jit(solution)/shard_map/while/body/eval_jaxpr/cond/branch_6_fun/ppermute | solution.py:167
  47.2 3.7 %collective-permute-start.47 = (f32[8,128]{1,0:T(8,128)S(1)}, f32[8,128]{1,0:T(8,128)S(1)}, u32[]{:S(2)}, u32[]{:S(2)}) collective-permute-start(f32[8,128]{1,0:T(8,128)S(1)} %maximum_maximum_fusion.6.m0), channel_id=1, source_target_pairs={{0,2},{1,3},{2,0},{3,1},{4,6},{5,7},{6,4},{7,5},{8,10},{9,11},{10,... | collective-permute-start | bytes 12296 | tf_op jit(solution)/shard_map/while/body/eval_jaxpr/cond/branch_6_fun/ppermute | solution.py:167
  48.9 2.1 %collective-permute-start.46 = (f32[8,128]{1,0:T(8,128)S(1)}, f32[8,128]{1,0:T(8,128)S(1)}, u32[]{:S(2)}, u32[]{:S(2)}) collective-permute-start(f32[8,128]{1,0:T(8,128)S(1)} %maximum_maximum_fusion.6.m0), channel_id=1, source_target_pairs={{0,1},{1,0},{2,3},{3,2},{4,5},{5,4},{6,7},{7,6},{8,9},{9,8},{10,11... | collective-permute-start | bytes 12296 | tf_op jit(solution)/shard_map/while/body/eval_jaxpr/cond/branch_6_fun/ppermute | solution.py:167
  49.4 8.7 %collective-permute-start.42 = (f32[512,128]{1,0:T(8,128)S(1)}, f32[512,128]{1,0:T(8,128)S(1)}, u32[]{:S(2)}, u32[]{:S(2)}) collective-permute-start(f32[512,128]{1,0:T(8,128)S(1)} %branch_6_fun.4), channel_id=1, source_target_pairs={{0,28},{4,0},{8,4},{12,8},{16,12},{20,16},{24,20},{28,24},{1,29},{... | collective-permute-start | bytes 786440 | tf_op jit(solution)/shard_map/while/body/eval_jaxpr/cond/branch_6_fun/ppermute | solution.py:163
  58.7 1.3 %collective-permute-start.49 = (f32[136,128]{1,0:T(8,128)S(1)}, f32[136,128]{1,0:T(8,128)S(1)}, u32[]{:S(2)}, u32[]{:S(2)}) collective-permute-start(f32[136,128]{1,0:T(8,128)S(1)} %get-tuple-element.362), channel_id=1, source_target_pairs={{0,1},{1,0},{2,3},{3,2},{4,5},{5,4},{6,7},{7,6},{8,9},{9,8},{10,11... | collective-permute-start | bytes 208904 | tf_op jit(solution)/shard_map/while/body/eval_jaxpr/ppermute | solution.py:167
  60.1 4.4 %collective-permute-start.50 = (f32[136,128]{1,0:T(8,128)S(1)}, f32[136,128]{1,0:T(8,128)S(1)}, u32[]{:S(2)}, u32[]{:S(2)}) collective-permute-start(f32[136,128]{1,0:T(8,128)S(1)} %add.57.g0), channel_id=1, source_target_pairs={{0,2},{1,3},{2,0},{3,1},{4,6},{5,7},{6,4},{7,5},{8,10},{9,11},{10,... | collective-permute-start | bytes 208904 | tf_op jit(solution)/shard_map/while/body/eval_jaxpr/ppermute | solution.py:167
  64.8 3.9 %collective-permute-start.10 = (f32[8,128]{1,0:T(8,128)S(1)}, f32[8,128]{1,0:T(8,128)S(1)}, u32[]{:S(2)}, u32[]{:S(2)}) collective-permute-start(f32[8,128]{1,0:T(8,128)S(1)} %get-tuple-element.127), channel_id=1, source_target_pairs={{0,8},{4,12},{8,0},{12,4},{16,24},{20,28},{24,16},{28,20},{1,17},{... | collective-permute-start | bytes 12296 | tf_op jit(solution)/shard_map/while/body/eval_jaxpr/cond/branch_1_fun/ppermute | solution.py:196
  64.9 3.8 %collective-permute-start.9 = (f32[8,128]{1,0:T(8,128)S(1)}, f32[8,128]{1,0:T(8,128)S(1)}, u32[]{:S(2)}, u32[]{:S(2)}) collective-permute-start(f32[8,128]{1,0:T(8,128)S(1)} %get-tuple-element.127), channel_id=1, source_target_pairs={{0,4},{4,0},{8,12},{12,8},{16,20},{20,16},{24,28},{28,24},{1,13},{... | collective-permute-start | bytes 12296 | tf_op jit(solution)/shard_map/while/body/eval_jaxpr/cond/branch_1_fun/ppermute | solution.py:196
  66.8 14.0 %collective-permute-start.8 = (f32[640,128]{1,0:T(8,128)S(1)}, f32[640,128]{1,0:T(8,128)S(1)}, u32[]{:S(2)}, u32[]{:S(2)}) collective-permute-start(f32[640,128]{1,0:T(8,128)S(1)} %get-tuple-element.126), channel_id=1, source_target_pairs={{0,8},{4,12},{8,16},{12,20},{16,24},{20,28},{24,0},{28,4},{1,9},{5... | collective-permute-start | bytes 983048 | tf_op jit(solution)/shard_map/while/body/eval_jaxpr/cond/branch_1_fun/ppermute | solution.py:163
  68.7 7.5 %collective-permute-start.13 = (f32[8,128]{1,0:T(8,128)S(1)}, f32[8,128]{1,0:T(8,128)S(1)}, u32[]{:S(2)}, u32[]{:S(2)}) collective-permute-start(f32[8,128]{1,0:T(8,128)S(1)} %maximum_maximum_fusion.1.m0), channel_id=1, source_target_pairs={{0,3},{1,2},{2,1},{3,0},{4,7},{5,6},{6,5},{7,4},{8,11},{9,10},{10,... | collective-permute-start | bytes 12296 | tf_op jit(solution)/shard_map/while/body/eval_jaxpr/cond/branch_1_fun/ppermute | solution.py:167
  74.9 3.6 %collective-permute-start.12 = (f32[8,128]{1,0:T(8,128)S(1)}, f32[8,128]{1,0:T(8,128)S(1)}, u32[]{:S(2)}, u32[]{:S(2)}) collective-permute-start(f32[8,128]{1,0:T(8,128)S(1)} %maximum_maximum_fusion.1.m0), channel_id=1, source_target_pairs={{0,2},{1,3},{2,0},{3,1},{4,6},{5,7},{6,4},{7,5},{8,10},{9,11},{10,... | collective-permute-start | bytes 12296 | tf_op jit(solution)/shard_map/while/body/eval_jaxpr/cond/branch_1_fun/ppermute | solution.py:167
  74.9 3.6 %collective-permute-start.11 = (f32[8,128]{1,0:T(8,128)S(1)}, f32[8,128]{1,0:T(8,128)S(1)}, u32[]{:S(2)}, u32[]{:S(2)}) collective-permute-start(f32[8,128]{1,0:T(8,128)S(1)} %maximum_maximum_fusion.1.m0), channel_id=1, source_target_pairs={{0,1},{1,0},{2,3},{3,2},{4,5},{5,4},{6,7},{7,6},{8,9},{9,8},{10,11... | collective-permute-start | bytes 12296 | tf_op jit(solution)/shard_map/while/body/eval_jaxpr/cond/branch_1_fun/ppermute | solution.py:167
  75.5 10.4 %collective-permute-start.7 = (f32[512,128]{1,0:T(8,128)S(1)}, f32[512,128]{1,0:T(8,128)S(1)}, u32[]{:S(2)}, u32[]{:S(2)}) collective-permute-start(f32[512,128]{1,0:T(8,128)S(1)} %branch_1_fun.4), channel_id=1, source_target_pairs={{0,8},{4,12},{8,16},{12,20},{16,24},{20,28},{24,0},{28,4},{1,9},{5... | collective-permute-start | bytes 786440 | tf_op jit(solution)/shard_map/while/body/eval_jaxpr/cond/branch_1_fun/ppermute | solution.py:163
  86.6 1.3 %collective-permute-start.49 = (f32[136,128]{1,0:T(8,128)S(1)}, f32[136,128]{1,0:T(8,128)S(1)}, u32[]{:S(2)}, u32[]{:S(2)}) collective-permute-start(f32[136,128]{1,0:T(8,128)S(1)} %get-tuple-element.362), channel_id=1, source_target_pairs={{0,1},{1,0},{2,3},{3,2},{4,5},{5,4},{6,7},{7,6},{8,9},{9,8},{10,11... | collective-permute-start | bytes 208904 | tf_op jit(solution)/shard_map/while/body/eval_jaxpr/ppermute | solution.py:167
  87.9 4.6 %collective-permute-start.50 = (f32[136,128]{1,0:T(8,128)S(1)}, f32[136,128]{1,0:T(8,128)S(1)}, u32[]{:S(2)}, u32[]{:S(2)}) collective-permute-start(f32[136,128]{1,0:T(8,128)S(1)} %add.57.g0), channel_id=1, source_target_pairs={{0,2},{1,3},{2,0},{3,1},{4,6},{5,7},{6,4},{7,5},{8,10},{9,11},{10,... | collective-permute-start | bytes 208904 | tf_op jit(solution)/shard_map/while/body/eval_jaxpr/ppermute | solution.py:167
  92.9 4.2 %collective-permute-start.17 = (f32[8,128]{1,0:T(8,128)S(1)}, f32[8,128]{1,0:T(8,128)S(1)}, u32[]{:S(2)}, u32[]{:S(2)}) collective-permute-start(f32[8,128]{1,0:T(8,128)S(1)} %get-tuple-element.142), channel_id=1, source_target_pairs={{0,8},{4,12},{8,0},{12,4},{16,24},{20,28},{24,16},{28,20},{1,17},{... | collective-permute-start | bytes 12296 | tf_op jit(solution)/shard_map/while/body/eval_jaxpr/cond/branch_2_fun/ppermute | solution.py:196
  93.0 4.4 %collective-permute-start.16 = (f32[8,128]{1,0:T(8,128)S(1)}, f32[8,128]{1,0:T(8,128)S(1)}, u32[]{:S(2)}, u32[]{:S(2)}) collective-permute-start(f32[8,128]{1,0:T(8,128)S(1)} %get-tuple-element.142), channel_id=1, source_target_pairs={{0,4},{4,0},{8,12},{12,8},{16,20},{20,16},{24,28},{28,24},{1,13},{... | collective-permute-start | bytes 12296 | tf_op jit(solution)/shard_map/while/body/eval_jaxpr/cond/branch_2_fun/ppermute | solution.py:196
  95.8 23.8 %collective-permute-start.15 = (f32[640,128]{1,0:T(8,128)S(1)}, f32[640,128]{1,0:T(8,128)S(1)}, u32[]{:S(2)}, u32[]{:S(2)}) collective-permute-start(f32[640,128]{1,0:T(8,128)S(1)} %get-tuple-element.141), channel_id=1, source_target_pairs={{0,12},{4,16},{8,20},{12,24},{16,28},{20,0},{24,4},{28,8},{1,13},{... | collective-permute-start | bytes 983048 | tf_op jit(solution)/shard_map/while/body/eval_jaxpr/cond/branch_2_fun/ppermute | solution.py:163
  97.4 6.1 %collective-permute-start.20 = (f32[8,128]{1,0:T(8,128)S(1)}, f32[8,128]{1,0:T(8,128)S(1)}, u32[]{:S(2)}, u32[]{:S(2)}) collective-permute-start(f32[8,128]{1,0:T(8,128)S(1)} %maximum_maximum_fusion.2.m0), channel_id=1, source_target_pairs={{0,3},{1,2},{2,1},{3,0},{4,7},{5,6},{6,5},{7,4},{8,11},{9,10},{10,... | collective-permute-start | bytes 12296 | tf_op jit(solution)/shard_map/while/body/eval_jaxpr/cond/branch_2_fun/ppermute | solution.py:167
  99.5 4.0 %collective-permute-start.19 = (f32[8,128]{1,0:T(8,128)S(1)}, f32[8,128]{1,0:T(8,128)S(1)}, u32[]{:S(2)}, u32[]{:S(2)}) collective-permute-start(f32[8,128]{1,0:T(8,128)S(1)} %maximum_maximum_fusion.2.m0), channel_id=1, source_target_pairs={{0,2},{1,3},{2,0},{3,1},{4,6},{5,7},{6,4},{7,5},{8,10},{9,11},{10,... | collective-permute-start | bytes 12296 | tf_op jit(solution)/shard_map/while/body/eval_jaxpr/cond/branch_2_fun/ppermute | solution.py:167
  100.7 2.8 %collective-permute-start.18 = (f32[8,128]{1,0:T(8,128)S(1)}, f32[8,128]{1,0:T(8,128)S(1)}, u32[]{:S(2)}, u32[]{:S(2)}) collective-permute-start(f32[8,128]{1,0:T(8,128)S(1)} %maximum_maximum_fusion.2.m0), channel_id=1, source_target_pairs={{0,1},{1,0},{2,3},{3,2},{4,5},{5,4},{6,7},{7,6},{8,9},{9,8},{10,11... | collective-permute-start | bytes 12296 | tf_op jit(solution)/shard_map/while/body/eval_jaxpr/cond/branch_2_fun/ppermute | solution.py:167
  101.2 22.2 %collective-permute-start.14 = (f32[512,128]{1,0:T(8,128)S(1)}, f32[512,128]{1,0:T(8,128)S(1)}, u32[]{:S(2)}, u32[]{:S(2)}) collective-permute-start(f32[512,128]{1,0:T(8,128)S(1)} %branch_2_fun.4), channel_id=1, source_target_pairs={{0,12},{4,16},{8,20},{12,24},{16,28},{20,0},{24,4},{28,8},{1,13},{... | collective-permute-start | bytes 786440 | tf_op jit(solution)/shard_map/while/body/eval_jaxpr/cond/branch_2_fun/ppermute | solution.py:163
